TPU v7x, 512 devices: a whole 4x4x16 slice. The times are simulated.
512 devices in a mesh: ctx: 16 (over x, y), exp: 32 (over z, core).
Axes of the slice: x: 4, y: 4, z: 16, core: 2. Of those that a mesh axis runs over, the one named last changes fastest.
Arguments:
- query_matrix_rows: bfloat16 [16384, 4096], P('ctx', 'exp'), may hold values from -6 to 6
- key_matrix_rows: bfloat16 [16384, 4096], P('ctx', 'exp'), may hold values from -6 to 6
- value_matrix_rows: bfloat16 [16384, 4096], P('ctx', 'exp'), may hold values from -6 to 6
- strength: float32 [32, 16384], P('exp', 'ctx'), may hold values from 0.00390625 to 0.0234375
- channel_forget_rate: float32 [32, 128], P('exp'), may hold values from 3.0517578e-06 to 0.03125
- forget_rate_factor: float32 [32, 16384], P('exp', 'ctx'), may hold values from 0.5 to 2
- extra_log_decay: float32 [32, 16384], P('exp', 'ctx'), may hold values from 0 to 0.69
- initial_head_state: float32 [32, 128, 128], P('exp'), may hold values from -4 to 4
- other_residual_input: bfloat16 [65536, 1152], P(('ctx', 'exp')), may hold values from -75 to 75
- token_segment_index: int32 [65536], P(('ctx', 'exp')), may hold values from 0 to 2047, never falling along the last dimension, each value on 1 to 128 neighbouring positions
- routes: int32 [65536, 8], P(('ctx', 'exp')), may hold values from 0 to 31, all different within a row; in each aligned block of 128 rows (0 to 127, 128 to 255, ...) at most 40 rows name the same one
- modality_norm_gain: float32 [3, 1152], replicated, may hold values from 0.1 to 1.9
- router_projection_weight: bfloat16 [1152, 32], replicated, may hold values from -0.1875 to 0.1875
- expert_gate_weight: bfloat16 [32, 1152, 512], P('exp', 'ctx'), may hold values from -0.1875 to 0.1875
- expert_up_weight: bfloat16 [32, 1152, 512], P('exp', 'ctx'), may hold values from -0.1875 to 0.1875
- expert_down_weight: bfloat16 [32, 512, 1152], P('exp', 'ctx'), may hold values from -0.25 to 0.25
Outputs:
- delta_attention_output: bfloat16 [16384, 4096], P('ctx', 'exp')
- context_group_state: float32 [16, 32, 128, 128], P('ctx', 'exp')
- mixer_out: bfloat16 [65536, 1152], P(('ctx', 'exp'))
Inputs may be any that keep to these rules, and one draw needn't show every extreme that they name: `routes`: in each aligned block of 128 rows (the rows of one device) no expert is named by more than 40 rows, a bound that some block reaches. A row names 8 different experts. `token_segment_index`: never falling along the tokens.
All inputs are finite; a program needn't handle non-finite values.
Results may differ from a plain program's by a relative error of at most 0.0077.
Values may be sent and summed in bfloat16 or wider, within the bound.
A program may use at most 64 MiB of HBM per device.

v0:
```python
import jax
import jax.numpy as jnp
from jax import lax
from jax.sharding import PartitionSpec as P

HD = 128
MODAL = 3
STRIDE_POSITIONS = 256
CAP = 40


exact = lax.Precision.HIGHEST
route_scale = 2.446
norm_eps = 1e-06


def shifted(value, axis, steps):
    count = lax.axis_size(axis)
    initial, last = (max(0, -steps), min(count, count - steps))
    return lax.ppermute(value, axis, [(source, source + steps) for source in range(initial, last)])


def unit_rows(values):
    return values * lax.rsqrt(jnp.sum(values * values, axis=-1, keepdims=True) + norm_eps)


def span_terms(query_unit, key_unit, values, strengths, summed_fading_exponent):
    length = query_unit.shape[2]
    head_dim = values.shape[-1]
    cumulative = jnp.cumsum(summed_fading_exponent, axis=2)
    final_log = cumulative[:, :, length - 1 :, :]
    key_grown = key_unit * jnp.exp(cumulative)
    key_shrunk = key_unit * jnp.exp(-cumulative)
    query_grown = query_unit * jnp.exp(cumulative)
    key_scores = jnp.einsum("hntc,hnsc->hnts", key_grown, key_shrunk, precision=exact)
    query_scores = jnp.einsum("hntc,hnsc->hnts", query_grown, key_shrunk, precision=exact)
    strict = jnp.tril(jnp.ones((length, length), jnp.float32), -1)
    inclusive = jnp.tril(jnp.ones((length, length), jnp.float32))
    system = jnp.eye(length, dtype=jnp.float32) + strengths[..., None] * key_scores * strict
    right_side = strengths[..., None] * jnp.concatenate([values, key_grown], axis=-1)
    solved = jax.scipy.linalg.solve_triangular(system, right_side, lower=True, unit_diagonal=True)
    written = solved[..., :head_dim]
    key_solved = solved[..., head_dim:]
    lower_scores = query_scores * inclusive
    inner_out = jnp.einsum("hnts,hnsd->hntd", lower_scores, written, precision=exact)
    reader = query_grown - jnp.einsum("hnts,hnsc->hntc", lower_scores, key_solved, precision=exact)
    key_end = key_unit * jnp.exp(final_log - cumulative)
    transition = jnp.exp(final_log)[:, :, 0, :, None] * jnp.eye(head_dim, dtype=jnp.float32)
    transition = transition - jnp.einsum("hnsc,hnsd->hncd", key_end, key_solved, precision=exact)
    addition = jnp.einsum("hnsc,hnsd->hncd", key_end, written, precision=exact)
    return (inner_out, reader, transition, addition)


def apply_map(mapping, target):
    return jnp.einsum("hce,hed->hcd", mapping, target, precision=exact)


def run_experts(arrived, gathered_gate, gathered_up, gathered_down):
    gate_acts = jnp.einsum(
        "slkd,ldf->slkf", arrived, gathered_gate, preferred_element_type=jnp.float32
    )
    up_acts = jnp.einsum("slkd,ldf->slkf", arrived, gathered_up, preferred_element_type=jnp.float32)
    hidden = (jax.nn.silu(gate_acts) * up_acts).astype(jnp.bfloat16)
    produced = jnp.einsum(
        "slkf,lfd->slkd", hidden, gathered_down, preferred_element_type=jnp.float32
    )
    return produced.astype(jnp.bfloat16)


def on_device(
    query_matrix_rows,
    key_matrix_rows,
    value_matrix_rows,
    strength,
    channel_forget_rate,
    forget_rate_factor,
    extra_log_decay,
    initial_head_state,
    other_residual_input,
    token_segment_index,
    routes,
    modality_norm_gain,
    router_projection_weight,
    expert_gate_weight,
    expert_up_weight,
    expert_down_weight,
):
    tokens, feature_width = query_matrix_rows.shape
    number_of_heads = feature_width // HD
    block_list = tokens // STRIDE_POSITIONS

    def heads_first(values):
        return (
            values.astype(jnp.float32)
            .reshape(block_list, STRIDE_POSITIONS, number_of_heads, HD)
            .transpose(2, 0, 1, 3)
        )

    query_unit = unit_rows(heads_first(query_matrix_rows))
    key_unit = unit_rows(heads_first(key_matrix_rows))
    values_now = heads_first(value_matrix_rows)
    strengths = strength.reshape(number_of_heads, block_list, STRIDE_POSITIONS)
    summed_fading_exponent = -(
        channel_forget_rate[:, None, None, :]
        * forget_rate_factor.reshape(number_of_heads, block_list, STRIDE_POSITIONS)[..., None]
        + extra_log_decay.reshape(number_of_heads, block_list, STRIDE_POSITIONS)[..., None]
    )
    inner_out, reader, transition, addition = span_terms(
        query_unit, key_unit, values_now, strengths, summed_fading_exponent
    )
    identity = jnp.broadcast_to(jnp.eye(HD, dtype=jnp.float32), (number_of_heads, HD, HD))
    zeros_state = jnp.zeros((number_of_heads, HD, HD), jnp.float32)

    def advance(carried, pieces_now):
        current, composed = carried
        inner_part, reader_part, trans_part, extra_part = pieces_now
        output_now = inner_part + jnp.einsum("htc,hcd->htd", reader_part, current, precision=exact)
        factor = jnp.einsum("htc,hcd->htd", reader_part, composed, precision=exact)
        following = apply_map(trans_part, current) + extra_part
        return ((following, apply_map(trans_part, composed)), (output_now, factor))

    pieces = tuple((jnp.moveaxis(item, 1, 0) for item in (inner_out, reader, transition, addition)))
    (local_end, transfer), (local_out, factors) = lax.scan(advance, (zeros_state, identity), pieces)
    is_first = lax.axis_index("ctx") == 0

    def relay_step(step_index, incoming):
        passed = shifted(apply_map(transfer, incoming) + local_end, "ctx", 1)
        return jnp.where(is_first, initial_head_state, passed)

    entering = lax.fori_loop(0, lax.axis_size("ctx") - 1, relay_step, initial_head_state)
    outputs = local_out + jnp.einsum("nhtc,hcd->nhtd", factors, entering, precision=exact)
    delta_attention_output = (
        outputs.transpose(0, 2, 1, 3).reshape(tokens, feature_width).astype(jnp.bfloat16)
    )
    context_group_state = (apply_map(transfer, entering) + local_end)[None]
    row_count, model_dim = other_residual_input.shape
    expert_count = router_projection_weight.shape[1]
    local_count = expert_gate_weight.shape[0]
    capacity = CAP
    modality = token_segment_index % MODAL
    modal_pick = (modality[:, None] == jnp.arange(MODAL)[None, :]).astype(jnp.float32)
    gains = jnp.dot(modal_pick, modality_norm_gain, precision=exact)
    stream = other_residual_input.astype(jnp.float32)
    normed = (
        stream * lax.rsqrt(jnp.mean(stream * stream, axis=1, keepdims=True) + norm_eps) * gains
    ).astype(jnp.bfloat16)
    logits = jnp.dot(normed, router_projection_weight, preferred_element_type=jnp.float32)
    chosen = routes[:, :, None] == jnp.arange(expert_count)[None, None, :]
    picked = jnp.sum(jnp.where(chosen, logits[:, None, :], 0.0), axis=2)
    scores = jax.nn.sigmoid(picked)
    weights = (route_scale * scores / jnp.sum(scores, axis=1, keepdims=True)).astype(jnp.bfloat16)
    per_expert = jnp.sum(jnp.where(chosen, weights.astype(jnp.float32)[:, :, None], 0.0), axis=1)
    hit_count = jnp.sum(chosen.astype(jnp.int32), axis=1)
    before = jnp.cumsum(hit_count, axis=0) - hit_count
    slot_ids = jnp.arange(capacity)
    matched = (hit_count[:, :, None] == 1) & (before[:, :, None] == slot_ids[None, None, :])
    mixing = jnp.where(matched, per_expert[:, :, None], 0.0).astype(jnp.bfloat16)
    gathered_gate, gathered_up, gathered_down = (
        lax.all_gather(expert_gate_weight, "ctx", axis=1, tiled=True),
        lax.all_gather(expert_up_weight, "ctx", axis=1, tiled=True),
        lax.all_gather(expert_down_weight, "ctx", axis=1, tiled=True),
    )
    slotted = matched.astype(jnp.bfloat16)
    outgoing = jnp.einsum(
        "rxp,rd->xpd", slotted, normed, preferred_element_type=jnp.float32
    ).astype(jnp.bfloat16)
    outgoing = outgoing.reshape(lax.axis_size("exp"), local_count, capacity, model_dim)
    produced = run_experts(
        lax.all_to_all(outgoing, "exp", split_axis=0, concat_axis=0, tiled=True),
        gathered_gate,
        gathered_up,
        gathered_down,
    )
    returned = lax.all_to_all(produced, "exp", split_axis=0, concat_axis=0, tiled=True)
    returned = returned.reshape(expert_count, capacity, model_dim)
    mixer_out = jnp.einsum(
        "rxp,xpd->rd", mixing, returned, preferred_element_type=jnp.float32
    ).astype(jnp.bfloat16)
    return (delta_attention_output, context_group_state, mixer_out)


def solution(mesh):
    placed = (
        P("ctx", "exp"),
        P("ctx", "exp"),
        P("ctx", "exp"),
        P("exp", "ctx"),
        P("exp", None),
        P("exp", "ctx"),
        P("exp", "ctx"),
        P("exp", None, None),
        P(("ctx", "exp"), None),
        P(("ctx", "exp")),
        P(("ctx", "exp"), None),
        P(),
        P(),
        P("exp", "ctx", None),
        P("exp", "ctx", None),
        P("exp", "ctx", None),
    )
    return jax.shard_map(
        on_device,
        mesh=mesh,
        in_specs=placed,
        out_specs=(P("ctx", "exp"), P("ctx", "exp", None, None), P(("ctx", "exp"), None)),
        check_vma=False,
    )
```

profile of v0, /device:TPU:2, one launch (start us, length us, event | category | flops | bytes accessed | tf_op | source)
XLA Modules:
  0.0 391.7 jit_solution(10717784949387794570)
XLA Ops:
  7.2 0.7 convert_reduce_fusion
  8.7 1.1 fusion.65
  10.1 1.4 fusion.40
  11.5 0.7 copy-done.1
  12.2 2.5 fusion.22
  14.8 15.7 %all-to-all-start = ((bf16[32,1,40,1152]{3,2,1,0:T(8,128)(2,1)}), bf16[32,1,40,1152]{3,2,1,0:T(8,128)(2,1)}, u32[]{:S(2)}, u32[]{:S(2)}) async-start(bf16[32,1,40,1152]{3,2,1,0:T(8,128)(2,1)} %fusion.22), calls=%async_computation | async-start | bytes 5898240 | tf_op jit(solution)/shard_map/all_to_all | solution.py:169
  30.6 0.7 all-gather.4.cloned.1.call-update
  31.3 0.7 all-gather.6.cloned.1.call-update
  32.1 0.7 all-gather.8.cloned.1.call-update
  37.0 0.8 convert.4
  37.9 1.0 multiply_bitcast_fusion
  38.9 1.4 fusion.49
  40.4 4.0 %while.29 = (s32[]{:T(128)}, f32[4,256,256]{2,1,0:T(8,128)S(1)}, s32[2,2]{1,0:T(2,128)S(1)}, f32[2,4,128,128]{3,2,0,1:T(8,128)S(1)}, s32[]{:T(128)}) while((s32[]{:T(128)}, f32[4,256,256]{2,1,0:T(8,128)S(1)}, s32[2,2]{1,0:T(2,128)S(1)}, f32[2,4,128,128]{3,2,0,1:T(8,128)S(1)}, s32[]{:T(128)}) %tuple.57), condition=%wide.while_cond, body=%wide.while_body.sunk | while | flops 2 | bytes 524405 | solution.py:41
  41.0 1.4 bitcast_dynamic-update-slice_fusion.2
  43.0 1.4 bitcast_dynamic-update-slice_fusion.2
  44.4 79.3 %custom-call.4 = f32[4,2,128,128]{2,3,1,0:T(8,128)} custom-call(f32[4,2,128,128]{3,2,1,0:T(8,128)S(1)} %bitcast.326), custom_call_target="InvertDiagBlocksLowerTriangular" | custom-call | tf_op jit(solution)/shard_map/jit(_solve_triangular)/vmap()/triangular_solve | solution.py:41
  123.7 0.7 fusion.87
  124.4 1.4 maximum_multiply_fusion
  125.8 38.3 %all-to-all-done = bf16[32,1,40,1152]{3,2,1,0:T(8,128)(2,1)} async-done(((bf16[32,1,40,1152]{3,2,1,0:T(8,128)(2,1)}), bf16[32,1,40,1152]{3,2,1,0:T(8,128)(2,1)}, u32[]{:S(2)}, u32[]{:S(2)}) %all-to-all-start) | async-done | bytes 2949152 | tf_op jit(solution)/shard_map/all_to_all | solution.py:169
  164.1 5.6 %fusion.28 = f32[32,40,512]{2,1,0:T(8,128)} fusion(bf16[32,1,40,1152]{3,2,1,0:T(8,128)(2,1)} %all-to-all-done, bf16[1,1152,512]{2,1,0:T(8,128)(2,1)} %all-gather.4.cloned.1.call-done), kind=kOutput, calls=%fused_computation.39 | convolution fusion | flops 1509949440 | bytes 6750208 | tf_op jit(solution)/shard_map/slkd,ldf->slkf/dot_general | solution.py:59
  169.7 46.2 %all-gather.8.cloned.1.call-done = bf16[1,512,1152]{2,1,0:T(8,128)(2,1)} async-done(((bf16[1,32,1152]{2,1,0:T(8,128)(2,1)}), bf16[1,512,1152]{2,1,0:T(8,128)(2,1)}) %all-gather.8.cloned.1.call-update) | async-done | bytes 1179664 | tf_op jit(solution)/shard_map/all_gather | solution.py:161
  215.9 8.7 %fusion.23 = bf16[32,1,40,1152]{3,2,1,0:T(8,128)(2,1)} fusion(bf16[32,1,40,1152]{3,2,1,0:T(8,128)(2,1)} %all-to-all-done, f32[32,40,512]{2,1,0:T(8,128)} %fusion.28, bf16[1,512,1152]{2,1,0:T(8,128)(2,1)} %all-gather.8.cloned.1.call-done, bf16[1,1152,512]{2,1,0:T(8,128)(2,1)} %all-gather.6.cloned.1.call-done), kind=kOutput, calls=%fused_computation.34 | convolution fusion | flops 3025305600 | bytes 10878976 | tf_op jit(solution)/shard_map/slkf,lfd->slkd/dot_general | solution.py:64
  224.6 12.9 %all-to-all-start.1 = ((bf16[32,1,40,1152]{3,2,1,0:T(8,128)(2,1)}), bf16[32,1,40,1152]{3,2,1,0:T(8,128)(2,1)}, u32[]{:S(2)}, u32[]{:S(2)}) async-start(bf16[32,1,40,1152]{3,2,1,0:T(8,128)(2,1)} %fusion.23), calls=%async_computation.1 | async-start | bytes 5898240 | tf_op jit(solution)/shard_map/all_to_all | solution.py:174
  237.4 1.6 fusion.66
  240.5 1.2 convolution_multiply_fusion.1
  241.7 1.1 convolution_bitcast_fusion.4
  242.8 1.2 convolution_bitcast_fusion.5
  244.0 1.2 fusion.60
  245.3 1.1 fusion.54
  246.4 4.6 %while.27 = (s32[]{:T(128)}, f32[1,128,128]{2,1,0:T(8,128)S(1)}, f32[1,128,128]{2,1,0:T(8,128)S(1)}, f32[4,1,256,128]{2,3,0,1:T(8,128)S(1)}, f32[4,1,256,128]{3,...) while((s32[]{:T(128)}, f32[1,128,128]{2,1,0:T(8,128)S(1)}, ...), condition=%wide.region_5.6_spmd, body=%wide.region_4.5_spmd.sunk | while | flops 151044096 | bytes 2034805 | solution.py:123
  251.0 128.3 %while.28 = (s32[]{:T(128)}, f32[1,128,128]{2,1,0:T(8,128)S(1)}, pred[]{:T(512)}, f32[1,128,128]{2,1,0:T(8,128)S(1)}, f32[1,128,128]{2,1,0:T(8,128)S(1)}, /*index=5*/f32[1,128,128]{2,1,0:T(8,128)S(1)}, s32[]{:T(128)}) while((s32[]{:T(128)}, f32[1,128,128]{2,1,0:T(8,128)S(1)}, pred[]{:T(512)}, f32[1,128,128]{2,1,0:T(8,128)S(1)}, ...), condition=%wide.region_7.8_spmd, body=%wide.region_6.7_spmd.sunk | while | flops 25198592 | bytes 721014 | solution.py:130
  251.2 2.2 collective-permute-start
  253.4 6.1 %collective-permute-done = f32[1,128,128]{2,1,0:T(8,128)S(1)} collective-permute-done((f32[1,128,128]{2,1,0:T(8,128)S(1)}, f32[1,128,128]{2,1,0:T(8,128)S(1)}, u32[]{:S(2)}, u32[]{:S(2)}) %collective-permute-start) | collective-permute-done | bytes 65568 | tf_op jit(solution)/shard_map/while/body/eval_jaxpr/ppermute | solution.py:20
  259.7 1.9 collective-permute-start
  261.7 6.3 %collective-permute-done = f32[1,128,128]{2,1,0:T(8,128)S(1)} collective-permute-done((f32[1,128,128]{2,1,0:T(8,128)S(1)}, f32[1,128,128]{2,1,0:T(8,128)S(1)}, u32[]{:S(2)}, u32[]{:S(2)}) %collective-permute-start) | collective-permute-done | bytes 65568 | tf_op jit(solution)/shard_map/while/body/eval_jaxpr/ppermute | solution.py:20
  268.2 1.9 collective-permute-start
  270.2 6.3 %collective-permute-done = f32[1,128,128]{2,1,0:T(8,128)S(1)} collective-permute-done((f32[1,128,128]{2,1,0:T(8,128)S(1)}, f32[1,128,128]{2,1,0:T(8,128)S(1)}, u32[]{:S(2)}, u32[]{:S(2)}) %collective-permute-start) | collective-permute-done | bytes 65568 | tf_op jit(solution)/shard_map/while/body/eval_jaxpr/ppermute | solution.py:20
  276.8 1.9 collective-permute-start
  278.7 6.3 %collective-permute-done = f32[1,128,128]{2,1,0:T(8,128)S(1)} collective-permute-done((f32[1,128,128]{2,1,0:T(8,128)S(1)}, f32[1,128,128]{2,1,0:T(8,128)S(1)}, u32[]{:S(2)}, u32[]{:S(2)}) %collective-permute-start) | collective-permute-done | bytes 65568 | tf_op jit(solution)/shard_map/while/body/eval_jaxpr/ppermute | solution.py:20
  285.3 1.9 collective-permute-start
  287.2 6.3 %collective-permute-done = f32[1,128,128]{2,1,0:T(8,128)S(1)} collective-permute-done((f32[1,128,128]{2,1,0:T(8,128)S(1)}, f32[1,128,128]{2,1,0:T(8,128)S(1)}, u32[]{:S(2)}, u32[]{:S(2)}) %collective-permute-start) | collective-permute-done | bytes 65568 | tf_op jit(solution)/shard_map/while/body/eval_jaxpr/ppermute | solution.py:20
  293.8 1.9 collective-permute-start
  295.7 6.3 %collective-permute-done = f32[1,128,128]{2,1,0:T(8,128)S(1)} collective-permute-done((f32[1,128,128]{2,1,0:T(8,128)S(1)}, f32[1,128,128]{2,1,0:T(8,128)S(1)}, u32[]{:S(2)}, u32[]{:S(2)}) %collective-permute-start) | collective-permute-done | bytes 65568 | tf_op jit(solution)/shard_map/while/body/eval_jaxpr/ppermute | solution.py:20
  302.3 1.9 collective-permute-start
  304.2 6.3 %collective-permute-done = f32[1,128,128]{2,1,0:T(8,128)S(1)} collective-permute-done((f32[1,128,128]{2,1,0:T(8,128)S(1)}, f32[1,128,128]{2,1,0:T(8,128)S(1)}, u32[]{:S(2)}, u32[]{:S(2)}) %collective-permute-start) | collective-permute-done | bytes 65568 | tf_op jit(solution)/shard_map/while/body/eval_jaxpr/ppermute | solution.py:20
  310.8 1.9 collective-permute-start
  312.7 6.3 %collective-permute-done = f32[1,128,128]{2,1,0:T(8,128)S(1)} collective-permute-done((f32[1,128,128]{2,1,0:T(8,128)S(1)}, f32[1,128,128]{2,1,0:T(8,128)S(1)}, u32[]{:S(2)}, u32[]{:S(2)}) %collective-permute-start) | collective-permute-done | bytes 65568 | tf_op jit(solution)/shard_map/while/body/eval_jaxpr/ppermute | solution.py:20
  319.3 1.9 collective-permute-start
  321.2 7.0 %collective-permute-done = f32[1,128,128]{2,1,0:T(8,128)S(1)} collective-permute-done((f32[1,128,128]{2,1,0:T(8,128)S(1)}, f32[1,128,128]{2,1,0:T(8,128)S(1)}, u32[]{:S(2)}, u32[]{:S(2)}) %collective-permute-start) | collective-permute-done | bytes 65568 | tf_op jit(solution)/shard_map/while/body/eval_jaxpr/ppermute | solution.py:20
  328.5 1.9 collective-permute-start
  330.4 6.3 %collective-permute-done = f32[1,128,128]{2,1,0:T(8,128)S(1)} collective-permute-done((f32[1,128,128]{2,1,0:T(8,128)S(1)}, f32[1,128,128]{2,1,0:T(8,128)S(1)}, u32[]{:S(2)}, u32[]{:S(2)}) %collective-permute-start) | collective-permute-done | bytes 65568 | tf_op jit(solution)/shard_map/while/body/eval_jaxpr/ppermute | solution.py:20
  337.0 1.9 collective-permute-start
  338.9 6.3 %collective-permute-done = f32[1,128,128]{2,1,0:T(8,128)S(1)} collective-permute-done((f32[1,128,128]{2,1,0:T(8,128)S(1)}, f32[1,128,128]{2,1,0:T(8,128)S(1)}, u32[]{:S(2)}, u32[]{:S(2)}) %collective-permute-start) | collective-permute-done | bytes 65568 | tf_op jit(solution)/shard_map/while/body/eval_jaxpr/ppermute | solution.py:20
  345.5 1.9 collective-permute-start
  347.4 6.3 %collective-permute-done = f32[1,128,128]{2,1,0:T(8,128)S(1)} collective-permute-done((f32[1,128,128]{2,1,0:T(8,128)S(1)}, f32[1,128,128]{2,1,0:T(8,128)S(1)}, u32[]{:S(2)}, u32[]{:S(2)}) %collective-permute-start) | collective-permute-done | bytes 65568 | tf_op jit(solution)/shard_map/while/body/eval_jaxpr/ppermute | solution.py:20
  354.0 1.9 collective-permute-start
  355.9 6.3 %collective-permute-done = f32[1,128,128]{2,1,0:T(8,128)S(1)} collective-permute-done((f32[1,128,128]{2,1,0:T(8,128)S(1)}, f32[1,128,128]{2,1,0:T(8,128)S(1)}, u32[]{:S(2)}, u32[]{:S(2)}) %collective-permute-start) | collective-permute-done | bytes 65568 | tf_op jit(solution)/shard_map/while/body/eval_jaxpr/ppermute | solution.py:20
  362.5 1.9 collective-permute-start
  364.4 6.3 %collective-permute-done = f32[1,128,128]{2,1,0:T(8,128)S(1)} collective-permute-done((f32[1,128,128]{2,1,0:T(8,128)S(1)}, f32[1,128,128]{2,1,0:T(8,128)S(1)}, u32[]{:S(2)}, u32[]{:S(2)}) %collective-permute-start) | collective-permute-done | bytes 65568 | tf_op jit(solution)/shard_map/while/body/eval_jaxpr/ppermute | solution.py:20
  371.0 1.9 collective-permute-start
  372.9 6.3 %collective-permute-done = f32[1,128,128]{2,1,0:T(8,128)S(1)} collective-permute-done((f32[1,128,128]{2,1,0:T(8,128)S(1)}, f32[1,128,128]{2,1,0:T(8,128)S(1)}, u32[]{:S(2)}, u32[]{:S(2)}) %collective-permute-start) | collective-permute-done | bytes 65568 | tf_op jit(solution)/shard_map/while/body/eval_jaxpr/ppermute | solution.py:20
  380.0 0.8 copy.86
  381.2 0.8 fusion.62
  382.0 3.2 fusion.37
  (154 shorter events, 16.3 us)
Async XLA Ops:
  7.2 373.7 %copy-start = (bf16[1152,32]{0,1:T(8,128)(2,1)S(1)}, bf16[1152,32]{0,1:T(8,128)(2,1)}, u32[]{:S(2)}) copy-start(bf16[1152,32]{0,1:T(8,128)(2,1)} %param.32) | copy-start | bytes 221188
  11.5 0.7 copy-start.1
  14.7 18.5 %copy-start.13 = (f32[1,1024]{1,0:T(1,128)S(1)}, f32[1,1024]{1,0:T(1,128)}, u32[]{:S(2)}) copy-start(f32[1,1024]{1,0:T(1,128)} %param.25) | copy-start | bytes 12292
  14.7 19.2 %copy-start.14 = (f32[1,1024]{1,0:T(1,128)S(1)}, f32[1,1024]{1,0:T(1,128)}, u32[]{:S(2)}) copy-start(f32[1,1024]{1,0:T(1,128)} %param.26) | copy-start | bytes 12292
  14.7 19.9 %copy-start.16 = (f32[1,128]{1,0:T(1,128)S(1)}, f32[1,128]{1,0:T(1,128)}, u32[]{:S(2)}) copy-start(f32[1,128]{1,0:T(1,128)} %param.24) | copy-start | bytes 1540
  14.7 20.7 %copy-start.4 = (bf16[1024,128]{1,0:T(8,128)(2,1)S(1)}, bf16[1024,128]{1,0:T(8,128)(2,1)}, u32[]{:S(2)}) copy-start(bf16[1024,128]{1,0:T(8,128)(2,1)} %param.20) | copy-start | bytes 786436
  14.8 20.9 %copy-start.6 = (bf16[1024,128]{1,0:T(8,128)(2,1)S(1)}, bf16[1024,128]{1,0:T(8,128)(2,1)}, u32[]{:S(2)}) copy-start(bf16[1024,128]{1,0:T(8,128)(2,1)} %param.21) | copy-start | bytes 786436
  14.8 149.4 %all-to-all-start = ((bf16[32,1,40,1152]{3,2,1,0:T(8,128)(2,1)}), bf16[32,1,40,1152]{3,2,1,0:T(8,128)(2,1)}, u32[]{:S(2)}, u32[]{:S(2)}) async-start(bf16[32,1,40,1152]{3,2,1,0:T(8,128)(2,1)} %fusion.22), calls=%async_computation | async-start | bytes 5898240 | tf_op jit(solution)/shard_map/all_to_all | solution.py:169
  30.5 5.8 %copy-start.15 = (f32[1,1024]{1,0:T(1,128)S(1)}, f32[1,1024]{1,0:T(1,128)}, u32[]{:S(2)}) copy-start(f32[1,1024]{1,0:T(1,128)} %param.23) | copy-start | bytes 12292
  30.5 6.5 %copy-start.3 = (f32[1,128,128]{2,1,0:T(8,128)S(1)}, f32[1,128,128]{2,1,0:T(8,128)}, u32[]{:S(2)}) copy-start(f32[1,128,128]{2,1,0:T(8,128)} %param.27) | copy-start | bytes 196612
  30.5 6.5 %copy-start.11 = (bf16[1024,128]{1,0:T(8,128)(2,1)S(1)}, bf16[1024,128]{1,0:T(8,128)(2,1)}, u32[]{:S(2)}) copy-start(bf16[1024,128]{1,0:T(8,128)(2,1)} %param.22) | copy-start | bytes 786436
  30.5 95.3 %all-gather.4.cloned.1.call-start = ((), (), s32[]{:S(2)}) async-start(), calls=%async_computation.2 | async-start | bytes 1253376 | tf_op jit(solution)/shard_map/all_gather | solution.py:159
  31.3 138.4 %all-gather.6.cloned.1.call-start = ((), (), s32[]{:S(2)}) async-start(), calls=%async_computation.3 | async-start | bytes 1253376 | tf_op jit(solution)/shard_map/all_gather | solution.py:160
  32.0 183.9 %all-gather.8.cloned.1.call-start = ((), (), s32[]{:S(2)}) async-start(), calls=%async_computation.4 | async-start | bytes 1253376 | tf_op jit(solution)/shard_map/all_gather | solution.py:161
  224.6 157.4 %all-to-all-start.1 = ((bf16[32,1,40,1152]{3,2,1,0:T(8,128)(2,1)}), bf16[32,1,40,1152]{3,2,1,0:T(8,128)(2,1)}, u32[]{:S(2)}, u32[]{:S(2)}) async-start(bf16[32,1,40,1152]{3,2,1,0:T(8,128)(2,1)} %fusion.23), calls=%async_computation.1 | async-start | bytes 5898240 | tf_op jit(solution)/shard_map/all_to_all | solution.py:174
  237.4 2.3 copy-start.8
  239.1 1.4 copy-start.5
  239.1 1.4 copy-start.7
  244.0 2.4 copy-start.9
  244.0 2.4 copy-start.10
  251.0 129.8 %copy-start.2 = (bf16[128,1152]{1,0:T(8,128)(2,1)S(1)}, bf16[128,1152]{1,0:T(8,128)(2,1)}, u32[]{:S(2)}) copy-start(bf16[128,1152]{1,0:T(8,128)(2,1)} %copy-done.1) | copy-start | bytes 884740
  251.0 130.0 %copy-start.12 = (s32[128,8]{0,1:T(8,128)S(1)}, s32[128,8]{0,1:T(8,128)}, u32[]{:S(2)}) copy-start(s32[128,8]{0,1:T(8,128)} %param.30) | copy-start | bytes 12292
  251.2 8.3 %collective-permute-start = (f32[1,128,128]{2,1,0:T(8,128)S(1)}, f32[1,128,128]{2,1,0:T(8,128)S(1)}, u32[]{:S(2)}, u32[]{:S(2)}) collective-permute-start(f32[1,128,128]{2,1,0:T(8,128)S(1)} %fusion.140), channel_id=1, source_target_pairs={{0,32},{32,64},{64,96},{96,128},{128,160},{160,192},{192,224},{224... | collective-permute-start | bytes 196616 | tf_op jit(solution)/shard_map/while/body/eval_jaxpr/ppermute | solution.py:20
  259.7 8.3 %collective-permute-start = (f32[1,128,128]{2,1,0:T(8,128)S(1)}, f32[1,128,128]{2,1,0:T(8,128)S(1)}, u32[]{:S(2)}, u32[]{:S(2)}) collective-permute-start(f32[1,128,128]{2,1,0:T(8,128)S(1)} %fusion.140), channel_id=1, source_target_pairs={{0,32},{32,64},{64,96},{96,128},{128,160},{160,192},{192,224},{224... | collective-permute-start | bytes 196616 | tf_op jit(solution)/shard_map/while/body/eval_jaxpr/ppermute | solution.py:20
  268.2 8.3 %collective-permute-start = (f32[1,128,128]{2,1,0:T(8,128)S(1)}, f32[1,128,128]{2,1,0:T(8,128)S(1)}, u32[]{:S(2)}, u32[]{:S(2)}) collective-permute-start(f32[1,128,128]{2,1,0:T(8,128)S(1)} %fusion.140), channel_id=1, source_target_pairs={{0,32},{32,64},{64,96},{96,128},{128,160},{160,192},{192,224},{224... | collective-permute-start | bytes 196616 | tf_op jit(solution)/shard_map/while/body/eval_jaxpr/ppermute | solution.py:20
  276.8 8.3 %collective-permute-start = (f32[1,128,128]{2,1,0:T(8,128)S(1)}, f32[1,128,128]{2,1,0:T(8,128)S(1)}, u32[]{:S(2)}, u32[]{:S(2)}) collective-permute-start(f32[1,128,128]{2,1,0:T(8,128)S(1)} %fusion.140), channel_id=1, source_target_pairs={{0,32},{32,64},{64,96},{96,128},{128,160},{160,192},{192,224},{224... | collective-permute-start | bytes 196616 | tf_op jit(solution)/shard_map/while/body/eval_jaxpr/ppermute | solution.py:20
  285.3 8.3 %collective-permute-start = (f32[1,128,128]{2,1,0:T(8,128)S(1)}, f32[1,128,128]{2,1,0:T(8,128)S(1)}, u32[]{:S(2)}, u32[]{:S(2)}) collective-permute-start(f32[1,128,128]{2,1,0:T(8,128)S(1)} %fusion.140), channel_id=1, source_target_pairs={{0,32},{32,64},{64,96},{96,128},{128,160},{160,192},{192,224},{224... | collective-permute-start | bytes 196616 | tf_op jit(solution)/shard_map/while/body/eval_jaxpr/ppermute | solution.py:20
  293.8 8.3 %collective-permute-start = (f32[1,128,128]{2,1,0:T(8,128)S(1)}, f32[1,128,128]{2,1,0:T(8,128)S(1)}, u32[]{:S(2)}, u32[]{:S(2)}) collective-permute-start(f32[1,128,128]{2,1,0:T(8,128)S(1)} %fusion.140), channel_id=1, source_target_pairs={{0,32},{32,64},{64,96},{96,128},{128,160},{160,192},{192,224},{224... | collective-permute-start | bytes 196616 | tf_op jit(solution)/shard_map/while/body/eval_jaxpr/ppermute | solution.py:20
  302.3 8.3 %collective-permute-start = (f32[1,128,128]{2,1,0:T(8,128)S(1)}, f32[1,128,128]{2,1,0:T(8,128)S(1)}, u32[]{:S(2)}, u32[]{:S(2)}) collective-permute-start(f32[1,128,128]{2,1,0:T(8,128)S(1)} %fusion.140), channel_id=1, source_target_pairs={{0,32},{32,64},{64,96},{96,128},{128,160},{160,192},{192,224},{224... | collective-permute-start | bytes 196616 | tf_op jit(solution)/shard_map/while/body/eval_jaxpr/ppermute | solution.py:20
  310.8 8.3 %collective-permute-start = (f32[1,128,128]{2,1,0:T(8,128)S(1)}, f32[1,128,128]{2,1,0:T(8,128)S(1)}, u32[]{:S(2)}, u32[]{:S(2)}) collective-permute-start(f32[1,128,128]{2,1,0:T(8,128)S(1)} %fusion.140), channel_id=1, source_target_pairs={{0,32},{32,64},{64,96},{96,128},{128,160},{160,192},{192,224},{224... | collective-permute-start | bytes 196616 | tf_op jit(solution)/shard_map/while/body/eval_jaxpr/ppermute | solution.py:20
  319.3 8.9 %collective-permute-start = (f32[1,128,128]{2,1,0:T(8,128)S(1)}, f32[1,128,128]{2,1,0:T(8,128)S(1)}, u32[]{:S(2)}, u32[]{:S(2)}) collective-permute-start(f32[1,128,128]{2,1,0:T(8,128)S(1)} %fusion.140), channel_id=1, source_target_pairs={{0,32},{32,64},{64,96},{96,128},{128,160},{160,192},{192,224},{224... | collective-permute-start | bytes 196616 | tf_op jit(solution)/shard_map/while/body/eval_jaxpr/ppermute | solution.py:20
  328.5 8.3 %collective-permute-start = (f32[1,128,128]{2,1,0:T(8,128)S(1)}, f32[1,128,128]{2,1,0:T(8,128)S(1)}, u32[]{:S(2)}, u32[]{:S(2)}) collective-permute-start(f32[1,128,128]{2,1,0:T(8,128)S(1)} %fusion.140), channel_id=1, source_target_pairs={{0,32},{32,64},{64,96},{96,128},{128,160},{160,192},{192,224},{224... | collective-permute-start | bytes 196616 | tf_op jit(solution)/shard_map/while/body/eval_jaxpr/ppermute | solution.py:20
  337.0 8.3 %collective-permute-start = (f32[1,128,128]{2,1,0:T(8,128)S(1)}, f32[1,128,128]{2,1,0:T(8,128)S(1)}, u32[]{:S(2)}, u32[]{:S(2)}) collective-permute-start(f32[1,128,128]{2,1,0:T(8,128)S(1)} %fusion.140), channel_id=1, source_target_pairs={{0,32},{32,64},{64,96},{96,128},{128,160},{160,192},{192,224},{224... | collective-permute-start | bytes 196616 | tf_op jit(solution)/shard_map/while/body/eval_jaxpr/ppermute | solution.py:20
  345.5 8.3 %collective-permute-start = (f32[1,128,128]{2,1,0:T(8,128)S(1)}, f32[1,128,128]{2,1,0:T(8,128)S(1)}, u32[]{:S(2)}, u32[]{:S(2)}) collective-permute-start(f32[1,128,128]{2,1,0:T(8,128)S(1)} %fusion.140), channel_id=1, source_target_pairs={{0,32},{32,64},{64,96},{96,128},{128,160},{160,192},{192,224},{224... | collective-permute-start | bytes 196616 | tf_op jit(solution)/shard_map/while/body/eval_jaxpr/ppermute | solution.py:20
  354.0 8.3 %collective-permute-start = (f32[1,128,128]{2,1,0:T(8,128)S(1)}, f32[1,128,128]{2,1,0:T(8,128)S(1)}, u32[]{:S(2)}, u32[]{:S(2)}) collective-permute-start(f32[1,128,128]{2,1,0:T(8,128)S(1)} %fusion.140), channel_id=1, source_target_pairs={{0,32},{32,64},{64,96},{96,128},{128,160},{160,192},{192,224},{224... | collective-permute-start | bytes 196616 | tf_op jit(solution)/shard_map/while/body/eval_jaxpr/ppermute | solution.py:20
  362.5 8.3 %collective-permute-start = (f32[1,128,128]{2,1,0:T(8,128)S(1)}, f32[1,128,128]{2,1,0:T(8,128)S(1)}, u32[]{:S(2)}, u32[]{:S(2)}) collective-permute-start(f32[1,128,128]{2,1,0:T(8,128)S(1)} %fusion.140), channel_id=1, source_target_pairs={{0,32},{32,64},{64,96},{96,128},{128,160},{160,192},{192,224},{224... | collective-permute-start | bytes 196616 | tf_op jit(solution)/shard_map/while/body/eval_jaxpr/ppermute | solution.py:20
  371.0 8.3 %collective-permute-start = (f32[1,128,128]{2,1,0:T(8,128)S(1)}, f32[1,128,128]{2,1,0:T(8,128)S(1)}, u32[]{:S(2)}, u32[]{:S(2)}) collective-permute-start(f32[1,128,128]{2,1,0:T(8,128)S(1)} %fusion.140), channel_id=1, source_target_pairs={{0,32},{32,64},{64,96},{96,128},{128,160},{160,192},{192,224},{224... | collective-permute-start | bytes 196616 | tf_op jit(solution)/shard_map/while/body/eval_jaxpr/ppermute | solution.py:20
Sparse Core Ops, SparseCore 0:
  34.4 59.4 all-gather.3
  96.9 57.9 all-gather.5
  158.0 57.8 all-gather.7
where the time goes:
time: 393 us; the launch traced here: 392 us
  waiting for transfers between devices  182 us (46%)
  other arithmetic  89.7 us (23%)
  starting transfers between devices  57.8 us (15%)
  matrix products  40 us (10%)
  between operations  14.3 us (4%)
  local copies, waits for them, and re-layouts  6.95 us (2%)
    ppermute x15, waiting for transfers between devices, shifted(): lax.ppermute(value, axis, [(source, source + steps) for source in range(i...  95.5 us
    another operation x5, other arithmetic, span_terms(): jax.scipy.linalg.solve_triangular(system, right_side, lower=True, unit_di...  79.4 us
    all_gather x1, waiting for transfers between devices, on_device(): lax.all_gather(expert_down_weight, 'ctx', axis=1, tiled=True)  46.2 us
    all_to_all x1, waiting for transfers between devices, on_device(): lax.all_to_all(outgoing, 'exp', split_axis=0, concat_axis=0, tiled=True)  38.3 us
    ppermute x15, starting transfers between devices, shifted(): lax.ppermute(value, axis, [(source, source + steps) for source in range(i...  29.1 us
    all_to_all x1, starting transfers between devices, on_device(): lax.all_to_all(outgoing, 'exp', split_axis=0, concat_axis=0, tiled=True)  15.7 us
    all_to_all x1, starting transfers between devices, on_device(): lax.all_to_all(produced, 'exp', split_axis=0, concat_axis=0, tiled=True)  12.9 us
    dot_general x1, matrix products, run_experts(): jnp.einsum('slkf,lfd->slkd', hidden, gathered_down, preferred_element_typ...  8.66 us
  transfers between devices with their start and end apart: 20, of which 17 were waited for; matrix products, arithmetic and copies ran while one was open for 30% of the time, Pallas kernels for 0%

commit v1 on v0

v1 whole, which is shorter than its diff:
```python
import functools

import jax
import jax.numpy as jnp
from jax import lax
from jax.experimental import pallas as pl
from jax.experimental.pallas import tpu as pltpu
from jax.sharding import PartitionSpec as P

F32 = jnp.float32
BF = jnp.bfloat16
MESH = pl.DeviceIdType.MESH

C = 128
CHUNKS = 8
TOK = 128
CAP = 40
EXPERTS = 32
MODAL = 3
D = 1152
FE = 512
SIDE = 4
SHARDS = SIDE * SIDE
DEPTH = D // SHARDS
WIDTH = FE // SHARDS
WINDOW = 8
LOCAL = 4
route_scale = 2.446
norm_eps = 1e-06

SLOT = {4: 0, -3: 1, 3: 2, -2: 3, 2: 4, -1: 5, 1: 6, 0: 7}


def dn(a, b, ca, cb):
    return lax.dot_general(
        a.astype(BF), b.astype(BF), (((ca,), (cb,)), ((), ())), preferred_element_type=F32
    )


def split(a):
    high = a.astype(BF)
    return high, (a - high.astype(F32)).astype(BF)


def dot3(a, b):
    ah, al = split(a)
    bh, bl = split(b)
    return dn(ah, bh, 1, 0) + dn(ah, bl, 1, 0) + dn(al, bh, 1, 0)


def unit(v):
    return v * lax.rsqrt(jnp.sum(v * v, axis=-1, keepdims=True) + norm_eps)


def iotas(shape):
    return (
        lax.broadcasted_iota(jnp.int32, shape, 0),
        lax.broadcasted_iota(jnp.int32, shape, 1),
    )


def chunk_terms(n, q_ref, k_ref, v_ref, f_ref, x_ref, b_ref, rate_ref, readers, inner, added, decay):
    row, col = iotas((C, C))
    rows = pl.ds(pl.multiple_of(n * C, C), C)
    ku = unit(k_ref[rows, :].astype(F32))
    qu = unit(q_ref[rows, :].astype(F32))
    v = v_ref[rows, :].astype(F32)
    f = f_ref[pl.ds(n, 1), :]
    x = x_ref[pl.ds(n, 1), :]
    b = b_ref[pl.ds(n, 1), :]
    fc = jnp.sum(jnp.where(col <= row, f, 0.0), axis=1, keepdims=True)
    xc = jnp.sum(jnp.where(col <= row, x, 0.0), axis=1, keepdims=True)
    bc = jnp.sum(jnp.where(col == row, b, 0.0), axis=1, keepdims=True)
    cum = -(rate_ref[0:1, :] * fc + xc)
    last = cum[C - 1 : C, :]
    grown = jnp.exp(cum)
    kg = ku * grown
    ks = ku * jnp.exp(-cum)
    qg = qu * grown
    ke = ku * jnp.exp(last - cum)
    scores = dn(jnp.concatenate([kg, qg], 0), ks, 1, 1)
    a = jnp.where(col < row, scores[:C] * bc, 0.0)
    low = jnp.where(col <= row, scores[C:], 0.0)
    eye = jnp.where(col == row, 1.0, 0.0)
    inverse = eye - a
    square = dn(a, a, 1, 0)
    for level in range(6):
        if level < 5:
            r = dn(jnp.concatenate([inverse, square], 0), square, 1, 0)
            inverse = inverse + r[:C]
            square = r[C:]
        else:
            inverse = inverse + dn(inverse, square, 1, 0)
    solved = dn(inverse, jnp.concatenate([v * bc, kg * bc], 1), 1, 0)
    r1 = dn(low, solved, 1, 0)
    r2 = dn(ke, solved, 0, 0)
    inner[n] = r1[:, :C]
    readers[n] = jnp.concatenate([(qg - r1[:, C:]).astype(BF), r2[:, C:].astype(BF)], 0)
    added[n] = r2[:, :C]
    column = jnp.sum(jnp.where(col == row, jnp.exp(last), 0.0), axis=1, keepdims=True)
    decay[n] = jnp.broadcast_to(column, (C, C))


def kernel(
    q_ref, k_ref, v_ref, b_ref, rate_ref, f_ref, x_ref, s0_ref, res_ref, seg_ref, routes_ref,
    gain_ref, router_ref, gate_ref, up_ref, down_ref,
    att_ref, state_ref, mix_ref,
    gs, us, wg, wu, wd, relay_g, relay_d, tok, table, slot_ids, slot_w, xin, eo, contrib, rs_out,
    rs_in, readers, inner, added, decay, gmap, rowmaps, colmaps, state, send_sem, recv_sem, loc_sem,
):
    ctx = lax.axis_index("ctx")
    own = lax.axis_index("exp")
    px, py = ctx // SIDE, ctx % SIDE
    pz, core = own // 2, own % 2
    planes = EXPERTS // 2
    sense = 1 - 2 * core

    def along_z(steps):
        return (ctx, lax.rem(pz + sense * steps + planes, planes) * 2 + core)

    def along_x(steps):
        return (lax.rem(px + steps, SIDE) * SIDE + py, own)

    def along_y(steps):
        return (px * SIDE + lax.rem(py + steps, SIDE), own)

    sibling = (ctx, pz * 2 + 1 - core)
    ids = {}

    def remote(name, src, dst, device):
        k = ids.setdefault(name, len(ids))
        return pltpu.make_async_remote_copy(
            src_ref=src, dst_ref=dst, send_sem=send_sem.at[k], recv_sem=recv_sem.at[k],
            device_id=device, device_id_type=MESH,
        )

    started = []

    def go(copies):
        for one in copies:
            one.start()
        started.extend(copies)
        return copies

    def arrive(copies):
        for one in copies:
            one.wait_recv()

    shard_x = py * SIDE + px
    down_rows = pl.ds(pl.multiple_of(ctx * WIDTH, WIDTH), WIDTH)
    locals_ = [
        pltpu.make_async_copy(gate_ref.at[0], gs.at[0, shard_x], loc_sem.at[0]),
        pltpu.make_async_copy(up_ref.at[0], us.at[0, shard_x], loc_sem.at[1]),
        pltpu.make_async_copy(down_ref.at[0], wd.at[0, down_rows], loc_sem.at[2]),
    ]
    for one in locals_:
        one.start()

    barrier = pltpu.get_barrier_semaphore()
    partners = [along_z(t) for t in (1, -1, 4, -4)] + [sibling]
    partners += [along_x(t) for t in (1, 2, 3)] + [along_y(t) for t in (1, 2, 3)]
    for device in partners:
        pl.semaphore_signal(barrier, inc=1, device_id=device, device_id_type=MESH)
    pl.semaphore_wait(barrier, len(partners))

    hop1 = go([
        remote("bg1", gate_ref.at[0], relay_g.at[0], along_z(4)),
        remote("bu1", up_ref.at[0], relay_g.at[1], along_z(4)),
        remote("bd1", down_ref.at[0], relay_d, along_z(-4)),
    ])

    def first(r, g_src, u_src, d_src):
        copies = []
        for t in (1, 3, 2):
            copies.append(remote(f"g1{r}{t}", g_src, gs.at[r, shard_x], along_x(t)))
            if r == 0:
                copies.append(remote(f"u1{r}{t}", u_src, us.at[r, shard_x], along_x(t)))
            else:
                copies.append(remote(f"u1{r}{t}", u_src, us.at[r, ctx], along_y(t)))
            copies.append(remote(f"d1{r}{t}", d_src, wd.at[2 * r, down_rows], along_y(t)))
        return copies

    def second(r):
        copies = []
        by_x = pl.ds(py * SIDE, SIDE)
        by_y = pl.ds(px * SIDE, SIDE)
        block = pl.ds(pl.multiple_of(px * SIDE * WIDTH, SIDE * WIDTH), SIDE * WIDTH)
        for t in (1, 3, 2):
            copies.append(remote(f"g2{r}{t}", gs.at[r, by_x], gs.at[r, by_x], along_y(t)))
            if r == 0:
                copies.append(remote(f"u2{r}{t}", us.at[r, by_x], us.at[r, by_x], along_y(t)))
            else:
                copies.append(remote(f"u2{r}{t}", us.at[r, by_y], us.at[r, by_y], along_x(t)))
            copies.append(remote(f"d2{r}{t}", wd.at[2 * r, block], wd.at[2 * r, block], along_x(t)))
        return copies

    first_own = go(first(0, gate_ref.at[0], up_ref.at[0], down_ref.at[0]))

    row, col = iotas((C, C))
    stream = res_ref[...].astype(F32)
    scale = lax.rsqrt(jnp.mean(stream * stream, axis=1, keepdims=True) + norm_eps)
    seg = seg_ref[...].astype(F32)
    modality = seg - MODAL * jnp.floor((seg + 0.5) * (1.0 / MODAL))
    modality = jnp.sum(jnp.where(col == row, modality, 0.0), axis=1, keepdims=True)
    gains = jnp.where(
        modality == 0.0,
        gain_ref[0:1, :],
        jnp.where(modality == 1.0, gain_ref[1:2, :], gain_ref[2:3, :]),
    )
    normed = (stream * scale * gains).astype(BF)
    tok[SLOT[0]] = normed
    logits = dn(normed, router_ref[...], 1, 0)
    lane = lax.broadcasted_iota(jnp.int32, (TOK, EXPERTS), 1)
    hits = jnp.zeros((TOK, EXPERTS), F32)
    routes = routes_ref[...]
    for turn in range(8):
        hits = hits + jnp.where(routes[:, turn : turn + 1] == lane, 1.0, 0.0)
    scores = jnp.where(hits > 0.0, 1.0 / (1.0 + jnp.exp(-logits)), 0.0)
    weights = route_scale * scores / jnp.sum(scores, axis=1, keepdims=True)
    wide = jnp.concatenate([weights, jnp.zeros((TOK, C - EXPERTS), F32)], 1)
    table[SLOT[0]] = jnp.transpose(wide)[:EXPERTS].astype(BF)

    def token_step(way, k):
        near, far = SLOT[way * (k - 1)], SLOT[way * k]
        return [
            remote(f"t{way}{k}", tok.at[near], tok.at[far], along_z(way)),
            remote(f"w{way}{k}", table.at[near], table.at[far], along_z(way)),
        ]

    ahead = {1: go(token_step(1, 1))}
    behind = {1: go(token_step(-1, 1))}

    def pass_on(k):
        arrive(ahead[k])
        if k < 4:
            ahead[k + 1] = go(token_step(1, k + 1))
        if k <= 3:
            arrive(behind[k])
            if k < 3:
                behind[k + 1] = go(token_step(-1, k + 1))

    def chunks(lo, hi):
        def body(n, carry):
            chunk_terms(
                n, q_ref, k_ref, v_ref, f_ref, x_ref, b_ref, rate_ref, readers, inner, added, decay
            )
            return carry

        lax.fori_loop(lo, hi, body, 0)

    chunks(0, 2)
    arrive(hop1)
    here_g, here_u, here_d = gs.at[1, shard_x], us.at[1, ctx], wd.at[2, down_rows]
    hop2 = go([
        remote("bg2", relay_g.at[0], here_g, along_z(4)),
        remote("bu2", relay_g.at[1], here_u, along_z(4)),
        remote("bd2", relay_d, here_d, along_z(-4)),
    ])
    for one in locals_:
        one.wait()
    arrive(first_own)
    second_own = go(second(0))
    chunks(2, 4)
    pass_on(1)
    chunks(4, 6)
    arrive(hop2)
    first_far = go(first(1, here_g, here_u, here_d))
    chunks(6, 8)
    pass_on(2)

    gmap[...] = jnp.concatenate([jnp.zeros((C, C), F32), jnp.where(col == row, 1.0, 0.0)], 1)

    def grow(n, carry):
        d = decay[n]
        m = gmap[...]
        r = dn(readers[n, C:], m, 1, 0)
        gmap[...] = jnp.concatenate(
            [d * m[:, :C] - r[:, :C] + added[n], d * m[:, C:] - r[:, C:]], 1
        )
        return carry

    lax.fori_loop(0, CHUNKS, grow, 0)
    rowmaps[py] = gmap[...]
    row_copies = go([remote(f"r{t}", gmap, rowmaps.at[py], along_y(t)) for t in (1, 3, 2)])
    arrive(first_far)
    second_far = go(second(1))
    arrive(row_copies)
    whole = rowmaps[0]
    for t in range(1, SIDE):
        m = rowmaps[t]
        whole = dot3(m[:, C:], whole)
        whole = jnp.concatenate([whole[:, :C] + m[:, :C], whole[:, C:]], 1)
    colmaps[px] = whole
    col_copies = go([
        remote(f"c{t}", colmaps.at[px], colmaps.at[px], along_x(t)) for t in (1, 3, 2)
    ])
    pass_on(3)

    def merge(src, r, dst, x_first):
        def body(h, carry):
            parts = []
            for late in range(2):
                i = 2 * h + late
                place = (i % SIDE) * SIDE + i // SIDE if x_first else i
                parts.append(src[r, place].astype(F32))
            at = pl.ds(pl.multiple_of(h * 2 * DEPTH, 2 * DEPTH), 2 * DEPTH)
            dst[2 * r, at, :] = jnp.concatenate(parts, 0).astype(BF)
            return carry

        lax.fori_loop(0, SHARDS // 2, body, 0)

    def share(r):
        return go([
            remote(f"sg{r}", wg.at[2 * r], wg.at[2 * r + 1], sibling),
            remote(f"su{r}", wu.at[2 * r], wu.at[2 * r + 1], sibling),
            remote(f"sd{r}", wd.at[2 * r], wd.at[2 * r + 1], sibling),
        ])

    arrive(second_own)
    merge(gs, 0, wg, True)
    merge(us, 0, wu, True)
    share_own = share(0)
    arrive(col_copies)
    entering = s0_ref[0]
    for t in range(SIDE - 1):
        m = colmaps[t]
        entering = jnp.where(px > t, dot3(m[:, C:], entering) + m[:, :C], entering)
    for t in range(SIDE - 1):
        m = rowmaps[t]
        entering = jnp.where(py > t, dot3(m[:, C:], entering) + m[:, :C], entering)
    state[...] = entering

    def outputs(n, carry):
        s = state[...]
        r = dn(readers[n], s, 1, 0)
        att_ref[pl.ds(pl.multiple_of(n * C, C), C), :] = (inner[n] + r[:C]).astype(BF)
        state[...] = decay[n] * s - r[C:] + added[n]
        return carry

    lax.fori_loop(0, CHUNKS, outputs, 0)
    state_ref[0, 0] = state[...]
    pass_on(4)
    arrive(second_far)
    merge(gs, 1, wg, True)
    merge(us, 1, wu, False)
    share_far = share(1)

    upper = jnp.where(row <= col, 1.0, 0.0)
    pick_row, pick_col = iotas((8, EXPERTS))
    mine = []
    for r in range(2):
        plane = lax.rem(pz + 8 * r, planes)
        mine += [2 * plane + core, 2 * plane + 1 - core]
    select = jnp.zeros((8, EXPERTS), F32)
    for e in range(LOCAL):
        select = select + jnp.where((pick_row == e) & (pick_col == mine[e]), 1.0, 0.0)
    for slot in range(WINDOW):
        w = dn(select, table[slot], 1, 0)
        hit = w != 0.0
        place = dn(jnp.where(hit, 1.0, 0.0), upper, 1, 0)
        slot_ids[slot] = jnp.where(hit, place + (CAP * (slot % 2) - 1.0), -1.0)
        slot_w[slot] = w

    PAIR = 2 * CAP
    place_rows = lax.broadcasted_iota(jnp.int32, (PAIR, 2 * TOK), 0).astype(F32)

    def spread(pair, weighted):
        a, b = 2 * pair, 2 * pair + 1
        parts = []
        for e in range(LOCAL):
            ids_row = jnp.concatenate([slot_ids[a, e : e + 1, :], slot_ids[b, e : e + 1, :]], 1)
            if weighted:
                value = jnp.concatenate([slot_w[a, e : e + 1, :], slot_w[b, e : e + 1, :]], 1)
            else:
                value = 1.0
            parts.append(jnp.where(place_rows == ids_row, value, 0.0))
        return jnp.concatenate(parts, 0).astype(BF)

    def gather(group):
        for half in range(2):
            pair = 2 * group + half
            both = tok[2 * pair : 2 * pair + 2].reshape(2 * TOK, D)
            rows = dn(spread(pair, False), both, 1, 0).astype(BF)
            for e in range(LOCAL):
                xin[e, half * PAIR : (half + 1) * PAIR, :] = rows[e * PAIR : (e + 1) * PAIR]

    def experts():
        def body(e, carry):
            x = xin[e]
            g = dn(x, wg[e], 1, 0)
            u = dn(x, wu[e], 1, 0)
            hidden = (g / (1.0 + jnp.exp(-g)) * u).astype(BF)
            eo[e] = dn(hidden, wd[e], 1, 0).astype(BF)
            return carry

        lax.fori_loop(0, LOCAL, body, 0)

    def combine(group):
        for half in range(2):
            pair = 2 * group + half
            made = jnp.concatenate(
                [eo[e, half * PAIR : (half + 1) * PAIR, :] for e in range(LOCAL)], 0
            )
            both = dn(spread(pair, True), made, 0, 0)
            contrib[2 * pair] = both[:TOK].astype(BF)
            contrib[2 * pair + 1] = both[TOK:].astype(BF)

    gather(0)
    arrive(share_own)
    arrive(share_far)
    experts()
    combine(0)

    sums = {}

    def send_sum(distance):
        way = -1 if distance > 0 else 1
        at = SLOT[distance]
        last = 4 if distance > 0 else -3
        if distance == last:
            src = contrib.at[at]
        else:
            outer = sums[distance - way]
            arrive(outer)
            inbox = SLOT[distance - way]
            rs_out[at] = (contrib[at].astype(F32) + rs_in[inbox].astype(F32)).astype(BF)
            src = rs_out.at[at]
        sums[distance] = go([remote(f"s{distance}", src, rs_in.at[at], along_z(way))])

    send_sum(4)
    send_sum(-3)
    gather(1)
    experts()
    combine(1)
    send_sum(3)
    send_sum(-2)
    send_sum(2)
    send_sum(-1)
    send_sum(1)
    arrive(sums[-1])
    arrive(sums[1])
    mix_ref[...] = (
        contrib[SLOT[0]].astype(F32)
        + rs_in[SLOT[1]].astype(F32)
        + rs_in[SLOT[-1]].astype(F32)
    ).astype(BF)
    for one in started:
        one.wait_send()


COPIES = 6 + 36 + 14 + 6 + 6 + 7


def on_device(
    q, k, v, strength, rate, factor, extra, s0, residual, seg, routes, gain, router, gate, up, down
):
    vmem = pl.BlockSpec(memory_space=pltpu.VMEM)
    hbm = pl.BlockSpec(memory_space=pl.ANY)
    V = pltpu.VMEM
    return pl.pallas_call(
        kernel,
        out_shape=(
            jax.ShapeDtypeStruct((CHUNKS * C, C), BF),
            jax.ShapeDtypeStruct((1, 1, C, C), F32),
            jax.ShapeDtypeStruct((TOK, D), BF),
        ),
        in_specs=[vmem] * 13 + [hbm] * 3,
        out_specs=(vmem, vmem, vmem),
        scratch_shapes=[
            V((2, SHARDS, DEPTH, FE), BF),
            V((2, SHARDS, DEPTH, FE), BF),
            V((LOCAL, D, FE), BF),
            V((LOCAL, D, FE), BF),
            V((LOCAL, FE, D), BF),
            V((2, DEPTH, FE), BF),
            V((WIDTH, D), BF),
            V((WINDOW, TOK, D), BF),
            V((WINDOW, EXPERTS, TOK), BF),
            V((WINDOW, 8, TOK), F32),
            V((WINDOW, 8, TOK), F32),
            V((LOCAL, 4 * CAP, D), BF),
            V((LOCAL, 4 * CAP, D), BF),
            V((WINDOW, TOK, D), BF),
            V((WINDOW, TOK, D), BF),
            V((WINDOW, TOK, D), BF),
            V((CHUNKS, 2 * C, C), BF),
            V((CHUNKS, C, C), F32),
            V((CHUNKS, C, C), F32),
            V((CHUNKS, C, C), F32),
            V((C, 2 * C), F32),
            V((SIDE, C, 2 * C), F32),
            V((SIDE, C, 2 * C), F32),
            V((C, C), F32),
            pltpu.SemaphoreType.DMA((COPIES,)),
            pltpu.SemaphoreType.DMA((COPIES,)),
            pltpu.SemaphoreType.DMA((3,)),
        ],
        compiler_params=pltpu.CompilerParams(
            collective_id=0, has_side_effects=True, vmem_limit_bytes=58 << 20
        ),
        cost_estimate=pl.CostEstimate(
            flops=7_000_000_000, bytes_accessed=6_000_000, transcendentals=2_000_000
        ),
    )(
        q, k, v,
        strength.reshape(CHUNKS, C), rate, factor.reshape(CHUNKS, C), extra.reshape(CHUNKS, C),
        s0, residual, seg.reshape(1, TOK), routes, gain, router, gate, up, down,
    )


def solution(mesh):
    placed = (
        P("ctx", "exp"), P("ctx", "exp"), P("ctx", "exp"), P("exp", "ctx"), P("exp", None),
        P("exp", "ctx"), P("exp", "ctx"), P("exp", None, None), P(("ctx", "exp"), None),
        P(("ctx", "exp")), P(("ctx", "exp"), None), P(), P(),
        P("exp", "ctx", None), P("exp", "ctx", None), P("exp", "ctx", None),
    )
    return jax.shard_map(
        on_device,
        mesh=mesh,
        in_specs=placed,
        out_specs=(P("ctx", "exp"), P("ctx", "exp", None, None), P(("ctx", "exp"), None)),
        check_vma=False,
    )
```

time: 393 us -> 144 us (0.37)
  the two profiles are of different devices: /device:TPU:2 before, /device:TPU:1 now
where the time goes in v1:
time: 144 us; the launch traced here: 142 us
  Pallas kernels  136 us (94%)
  local copies, waits for them, and re-layouts  5.41 us (4%)
    pallas_call x1, Pallas kernels, on_device(): pl.pallas_call(kernel, out_shape=(jax.ShapeDtypeStruct((CHUNKS * C, C), B...  136 us
    unnamed x11, local copies, waits for them, and re-layouts  5.41 us

profile of v1, /device:TPU:1, one launch (start us, length us, event | category | flops | bytes accessed | tf_op | source)
XLA Modules:
  0.0 142.1 jit_solution(10400918202129830241)
XLA Ops:
  0.6 0.0 copy-start.1
  0.6 1.4 %copy.19.routes_ref = s32[128,8]{1,0:T(8,128)} copy(s32[128,8]{0,1:T(8,128)} %param.26) | data formatting | bytes 8192 | tf_op args[10]
  2.1 0.0 copy-done.1
  2.1 0.9 copy.20.router_ref
  3.0 136.0 %shard_map.175 = (bf16[1024,128]{1,0:T(8,128)(2,1)}, f32[1,1,128,128]{3,2,1,0:T(8,128)}, bf16[128,1152]{1,0:T(8,128)(2,1)}) custom-call(bf16[1024,128]{1,0:T(8,128)(2,1)} %q_ref.1, bf16[1024,128]{1,0:T(8,128)(2,1)} %k_ref.1, bf16[1024,128]{1,0:T(8,128)(2,1)} %v_ref.1, f32[8,128]{1,0:T(8,128)} %bitcast.4, f32[1,128]{1,0:T(1,128)} %rate_ref.1, ...), custom_call_target="tpu_custom_call" | custom-call | flops 7000000000 | bytes 6000000 | tf_op jit(solution)/shard_map/pallas_call | solution.py:460
  139.0 0.0 copy-start.2
  139.0 0.0 copy-start
  139.0 1.7 %copy.24 = bf16[1024,128]{1,0:T(8,128)(2,1)} copy(bf16[1024,128]{1,0:T(8,128)(2,1)} %get-tuple-element.6) | data formatting | bytes 524288
  140.7 0.0 copy-done.2
  140.7 0.6 copy.25
  141.4 0.0 copy-done
  141.4 0.7 copy.26
Async XLA Ops:
  0.6 1.5 %copy-start.1 = (bf16[1152,32]{0,1:T(8,128)(2,1)S(1)}, bf16[1152,32]{0,1:T(8,128)(2,1)}, u32[]{:S(2)}) copy-start(bf16[1152,32]{0,1:T(8,128)(2,1)} %param.28) | copy-start | bytes 221188
  139.0 1.7 %copy-start.2 = (f32[1,1,128,128]{3,2,1,0:T(8,128)S(1)}, f32[1,1,128,128]{3,2,1,0:T(8,128)}, u32[]{:S(2)}) copy-start(f32[1,1,128,128]{3,2,1,0:T(8,128)} %get-tuple-element.7) | copy-start | bytes 196612
  139.0 2.4 %copy-start = (bf16[128,1152]{1,0:T(8,128)(2,1)S(1)}, bf16[128,1152]{1,0:T(8,128)(2,1)}, u32[]{:S(2)}) copy-start(bf16[128,1152]{1,0:T(8,128)(2,1)} %get-tuple-element.8) | copy-start | bytes 884740

commit v2 on v1

v2 whole, which is shorter than its diff:
```python
import functools

import jax
import jax.numpy as jnp
from jax import lax
from jax.experimental import pallas as pl
from jax.experimental.pallas import tpu as pltpu
from jax.sharding import PartitionSpec as P

F32 = jnp.float32
BF = jnp.bfloat16
MESH = pl.DeviceIdType.MESH

C = 128
CHUNKS = 8
TOK = 128
CAP = 40
EXPERTS = 32
MODAL = 3
D = 1152
FE = 512
SIDE = 4
SHARDS = SIDE * SIDE
DEPTH = D // SHARDS
WIDTH = FE // SHARDS
WINDOW = 8
LOCAL = 4
route_scale = 2.446
norm_eps = 1e-06

SLOT = {4: 0, -3: 1, 3: 2, -2: 3, 2: 4, -1: 5, 1: 6, 0: 7}


def dn(a, b, ca, cb):
    return lax.dot_general(
        a.astype(BF), b.astype(BF), (((ca,), (cb,)), ((), ())), preferred_element_type=F32
    )


def split(a):
    high = a.astype(BF)
    return high, (a - high.astype(F32)).astype(BF)


def dot3(a, b):
    ah, al = split(a)
    bh, bl = split(b)
    return dn(ah, bh, 1, 0) + dn(ah, bl, 1, 0) + dn(al, bh, 1, 0)


def unit(v):
    return v * lax.rsqrt(jnp.sum(v * v, axis=-1, keepdims=True) + norm_eps)


def iotas(shape):
    return (
        lax.broadcasted_iota(jnp.int32, shape, 0),
        lax.broadcasted_iota(jnp.int32, shape, 1),
    )


def chunk_terms(n, q_ref, k_ref, v_ref, f_ref, x_ref, b_ref, rate_ref, readers, inner, added, decay):
    row, col = iotas((C, C))
    rows = pl.ds(pl.multiple_of(n * C, C), C)
    ku = unit(k_ref[rows, :].astype(F32))
    qu = unit(q_ref[rows, :].astype(F32))
    v = v_ref[rows, :].astype(F32)
    f = f_ref[pl.ds(n, 1), :]
    x = x_ref[pl.ds(n, 1), :]
    b = b_ref[pl.ds(n, 1), :]
    fc = jnp.sum(jnp.where(col <= row, f, 0.0), axis=1, keepdims=True)
    xc = jnp.sum(jnp.where(col <= row, x, 0.0), axis=1, keepdims=True)
    bc = jnp.sum(jnp.where(col == row, b, 0.0), axis=1, keepdims=True)
    cum = -(rate_ref[0:1, :] * fc + xc)
    last = cum[C - 1 : C, :]
    grown = jnp.exp(cum)
    kg = ku * grown
    ks = ku * jnp.exp(-cum)
    qg = qu * grown
    ke = ku * jnp.exp(last - cum)
    scores = dn(jnp.concatenate([kg, qg], 0), ks, 1, 1)
    a = jnp.where(col < row, scores[:C] * bc, 0.0)
    low = jnp.where(col <= row, scores[C:], 0.0)
    eye = jnp.where(col == row, 1.0, 0.0)
    inverse = eye - a
    square = dn(a, a, 1, 0)
    for level in range(6):
        if level < 5:
            r = dn(jnp.concatenate([inverse, square], 0), square, 1, 0)
            inverse = inverse + r[:C]
            square = r[C:]
        else:
            inverse = inverse + dn(inverse, square, 1, 0)
    solved = dn(inverse, jnp.concatenate([v * bc, kg * bc], 1), 1, 0)
    r1 = dn(low, solved, 1, 0)
    r2 = dn(ke, solved, 0, 0)
    inner[n] = r1[:, :C]
    readers[n] = jnp.concatenate([(qg - r1[:, C:]).astype(BF), r2[:, C:].astype(BF)], 0)
    added[n] = r2[:, :C]
    column = jnp.sum(jnp.where(col == row, jnp.exp(last), 0.0), axis=1, keepdims=True)
    decay[n] = jnp.broadcast_to(column, (C, C))


def kernel(
    q_ref, k_ref, v_ref, b_ref, rate_ref, f_ref, x_ref, s0_ref, res_ref, seg_ref, routes_ref,
    gain_ref, router_ref, gate_ref, up_ref, down_ref,
    att_ref, state_ref, mix_ref,
    gs, us, wg, wu, wd, tok, table, slot_ids, slot_w, xin, eo, contrib, rs_out,
    rs_in, readers, inner, added, decay, gmap, rowmaps, colmaps, state, send_sem, recv_sem, loc_sem,
):
    ctx = lax.axis_index("ctx")
    own = lax.axis_index("exp")
    px, py = ctx // SIDE, ctx % SIDE
    pz, core = own // 2, own % 2
    planes = EXPERTS // 2
    sense = 1 - 2 * core

    def along_z(steps):
        return (ctx, lax.rem(pz + sense * steps + planes, planes) * 2 + core)

    def along_x(steps):
        return (lax.rem(px + sense * steps + SIDE, SIDE) * SIDE + py, own)

    def along_y(steps):
        return (px * SIDE + lax.rem(py + sense * steps + SIDE, SIDE), own)

    def along_column(steps):
        return (lax.rem(px + steps, SIDE) * SIDE + py, own)

    def along_row(steps):
        return (px * SIDE + lax.rem(py + steps, SIDE), own)

    sibling = (ctx, pz * 2 + 1 - core)
    ids = {}

    def remote(name, src, dst, device):
        k = ids.setdefault(name, len(ids))
        return pltpu.make_async_remote_copy(
            src_ref=src, dst_ref=dst, send_sem=send_sem.at[k], recv_sem=recv_sem.at[k],
            device_id=device, device_id_type=MESH,
        )

    started = []

    def go(copies):
        for one in copies:
            one.start()
        started.extend(copies)
        return copies

    def arrive(copies):
        for one in copies:
            one.wait_recv()

    barrier = pltpu.get_barrier_semaphore()
    partners = [along_z(t) for t in (1, -1, 8)] + [sibling]
    partners += [along_column(t) for t in (1, 2, 3)] + [along_row(t) for t in (1, 2, 3)]
    for device in partners:
        pl.semaphore_signal(barrier, inc=1, device_id=device, device_id_type=MESH)
    pl.semaphore_wait(barrier, len(partners))

    HALF = FE // 2
    pieces = {}
    for r in range(2):
        pieces["g", r] = (
            lambda i, r=r: gs.at[r, i],
            lambda i, r=r: gs.at[r, pl.ds(i * SIDE, SIDE)],
            gate_ref.at[0], True,
        )
        for half in range(2):
            cols = pl.ds(half * HALF, HALF)
            pieces[f"u{half}", r] = (
                lambda i, r=r, cols=cols: us.at[r, i, :, cols],
                lambda i, r=r, cols=cols: us.at[r, pl.ds(i * SIDE, SIDE), :, cols],
                up_ref.at[0, :, cols], half == 0,
            )
        pieces["d", r] = (
            lambda i, r=r: wd.at[2 * r, pl.ds(pl.multiple_of(i * WIDTH, WIDTH), WIDTH)],
            lambda i, r=r: wd.at[
                2 * r, pl.ds(pl.multiple_of(i * SIDE * WIDTH, SIDE * WIDTH), SIDE * WIDTH)
            ],
            down_ref.at[0], False,
        )
    moves = {}

    def place(key):
        x_first = pieces[key][3]
        return (px, py, along_x, along_y) if x_first else (py, px, along_y, along_x)

    def near(key):
        one, block, given, x_first = pieces[key]
        a, b, axis, other = place(key)
        here = one(b * SIDE + a)
        src = given if key[1] == 0 else here
        moves[key] = [
            remote(f"{key}p", src, here, axis(1)), remote(f"{key}m", src, here, axis(-1))
        ]
        go(moves[key])

    def near_on(key):
        one, block, given, x_first = pieces[key]
        a, b, axis, other = place(key)
        arrive(moves[key][:1])
        from_behind = one(b * SIDE + lax.rem(a - sense + SIDE, SIDE))
        moves[key].append(remote(f"{key}f", from_behind, from_behind, axis(1)))
        go(moves[key][2:])

    def far(key):
        one, block, given, x_first = pieces[key]
        a, b, axis, other = place(key)
        arrive(moves[key][1:])
        line = block(b)
        moves[key] = [
            remote(f"{key}P", line, line, other(1)), remote(f"{key}M", line, line, other(-1))
        ]
        go(moves[key])

    def far_on(key):
        one, block, given, x_first = pieces[key]
        a, b, axis, other = place(key)
        arrive(moves[key][:1])
        line = block(lax.rem(b - sense + SIDE, SIDE))
        moves[key].append(remote(f"{key}F", line, line, other(1)))
        go(moves[key][2:])

    def complete(key):
        arrive(moves[key][1:])

    KINDS = ("g", "u0", "u1", "d")
    across = {}
    locals_ = []

    def cross(kind):
        one, block, given, x_first = pieces[kind, 1]
        a, b, axis, other = place((kind, 1))
        across[kind] = go([remote(f"{kind}z", given, one(b * SIDE + a), along_z(8))])

    for kind in KINDS:
        cross(kind)
    for n, kind in enumerate(KINDS):
        one, block, given, x_first = pieces[kind, 0]
        a, b, axis, other = place((kind, 0))
        near((kind, 0))
        locals_.append(pltpu.make_async_copy(given, one(b * SIDE + a), loc_sem.at[n]))
        locals_[-1].start()

    def each(step, r, kinds=KINDS):
        for kind in kinds:
            step((kind, r))

    def crossed_one(key):
        arrive(across[key[0]])
        near(key)

    row, col = iotas((C, C))
    stream = res_ref[...].astype(F32)
    scale = lax.rsqrt(jnp.mean(stream * stream, axis=1, keepdims=True) + norm_eps)
    seg = seg_ref[...].astype(F32)
    modality = seg - MODAL * jnp.floor((seg + 0.5) * (1.0 / MODAL))
    modality = jnp.sum(jnp.where(col == row, modality, 0.0), axis=1, keepdims=True)
    gains = jnp.where(
        modality == 0.0,
        gain_ref[0:1, :],
        jnp.where(modality == 1.0, gain_ref[1:2, :], gain_ref[2:3, :]),
    )
    normed = (stream * scale * gains).astype(BF)
    tok[SLOT[0]] = normed
    logits = dn(normed, router_ref[...], 1, 0)
    lane = lax.broadcasted_iota(jnp.int32, (TOK, EXPERTS), 1)
    hits = jnp.zeros((TOK, EXPERTS), F32)
    routes = routes_ref[...]
    for turn in range(8):
        hits = hits + jnp.where(routes[:, turn : turn + 1] == lane, 1.0, 0.0)
    scores = jnp.where(hits > 0.0, 1.0 / (1.0 + jnp.exp(-logits)), 0.0)
    weights = route_scale * scores / jnp.sum(scores, axis=1, keepdims=True)
    wide = jnp.concatenate([weights, jnp.zeros((TOK, C - EXPERTS), F32)], 1)
    table[SLOT[0]] = jnp.transpose(wide)[:EXPERTS].astype(BF)

    def token_step(way, k, half):
        src, dst = SLOT[way * (k - 1)], SLOT[way * k]
        part = pl.ds(half * (TOK // 2), TOK // 2)
        copies = []
        if half == 0:
            copies.append(remote(f"w{way}{k}", table.at[src], table.at[dst], along_z(way)))
        copies.append(
            remote(f"t{way}{k}{half}", tok.at[src, part], tok.at[dst, part], along_z(way))
        )
        return go(copies)

    hops = {}

    def first_hop():
        for half in range(2):
            for way in (1, -1):
                hops[way, 1, half] = token_step(way, 1, half)

    def pass_on(k):
        for half in range(2):
            for way, last in ((1, 4), (-1, 3)):
                if k <= last:
                    arrive(hops[way, k, half])
                if k < last:
                    hops[way, k + 1, half] = token_step(way, k + 1, half)

    def chunks(lo, hi):
        def body(n, carry):
            chunk_terms(
                n, q_ref, k_ref, v_ref, f_ref, x_ref, b_ref, rate_ref, readers, inner, added, decay
            )
            return carry

        lax.fori_loop(lo, hi, body, 0)

    def merge(src, r, dst, kinds):
        def body(h, carry):
            at = pl.ds(pl.multiple_of(h * 2 * DEPTH, 2 * DEPTH), 2 * DEPTH)
            for lo, hi, x_first in kinds:
                parts = []
                for late in range(2):
                    i = 2 * h + late
                    where = (i % SIDE) * SIDE + i // SIDE if x_first else i
                    parts.append(src[r, where, :, lo:hi].astype(F32))
                dst[2 * r, at, lo:hi] = jnp.concatenate(parts, 0).astype(BF)
            return carry

        lax.fori_loop(0, SHARDS // 2, body, 0)

    GATE_KINDS = [(0, FE, True)]
    UP_KINDS = [(0, HALF, True), (HALF, FE, False)]

    def share(kind, held, r):
        return go([remote(f"s{kind}{r}", held.at[2 * r], held.at[2 * r + 1], sibling)])

    def outputs(n, carry):
        s = state[...]
        r = dn(readers[n], s, 1, 0)
        att_ref[pl.ds(pl.multiple_of(n * C, C), C), :] = (inner[n] + r[:C]).astype(BF)
        state[...] = decay[n] * s - r[C:] + added[n]
        return carry

    upper = jnp.where(row <= col, 1.0, 0.0)
    pick_row, pick_col = iotas((8, EXPERTS))
    mine = []
    for r in range(2):
        plane = lax.rem(pz + 8 * r, planes)
        mine += [2 * plane + core, 2 * plane + 1 - core]
    select = jnp.zeros((8, EXPERTS), F32)
    for e in range(LOCAL):
        select = select + jnp.where((pick_row == e) & (pick_col == mine[e]), 1.0, 0.0)

    PAIR = 2 * CAP
    place_rows = lax.broadcasted_iota(jnp.int32, (PAIR, 2 * TOK), 0).astype(F32)

    def spread(pair, weighted):
        a, b = 2 * pair, 2 * pair + 1
        parts = []
        for e in range(LOCAL):
            ids_row = jnp.concatenate([slot_ids[a, e : e + 1, :], slot_ids[b, e : e + 1, :]], 1)
            if weighted:
                value = jnp.concatenate([slot_w[a, e : e + 1, :], slot_w[b, e : e + 1, :]], 1)
            else:
                value = 1.0
            parts.append(jnp.where(place_rows == ids_row, value, 0.0))
        return jnp.concatenate(parts, 0).astype(BF)

    def gather(group):
        for half in range(2):
            pair = 2 * group + half
            for slot in (2 * pair, 2 * pair + 1):
                w = dn(select, table[slot], 1, 0)
                hit = w != 0.0
                count = dn(jnp.where(hit, 1.0, 0.0), upper, 1, 0)
                slot_ids[slot] = jnp.where(hit, count + (CAP * (slot % 2) - 1.0), -1.0)
                slot_w[slot] = w
            both = tok[2 * pair : 2 * pair + 2].reshape(2 * TOK, D)
            rows = dn(spread(pair, False), both, 1, 0).astype(BF)
            for e in range(LOCAL):
                xin[e, pair * PAIR : (pair + 1) * PAIR, :] = rows[e * PAIR : (e + 1) * PAIR]

    def experts(lo, hi, first, last):
        def body(e, carry):
            x = xin[e, first:last, :]
            g = dn(x, wg[e], 1, 0)
            u = dn(x, wu[e], 1, 0)
            hidden = (g / (1.0 + jnp.exp(-g)) * u).astype(BF)
            eo[e, first:last, :] = dn(hidden, wd[e], 1, 0).astype(BF)
            return carry

        if hi - lo == 1:
            body(lo, 0)
        else:
            lax.fori_loop(lo, hi, body, 0)

    def combine(group):
        for half in range(2):
            pair = 2 * group + half
            made = jnp.concatenate(
                [eo[e, pair * PAIR : (pair + 1) * PAIR, :] for e in range(LOCAL)], 0
            )
            both = dn(spread(pair, True), made, 0, 0)
            contrib[2 * pair] = both[:TOK].astype(BF)
            contrib[2 * pair + 1] = both[TOK:].astype(BF)

    each(near_on, 0)
    chunks(0, 2)
    for one in locals_:
        one.wait()
    each(far, 0)
    chunks(2, 8)
    gmap[...] = jnp.concatenate([jnp.zeros((C, C), F32), jnp.where(col == row, 1.0, 0.0)], 1)

    def grow(n, carry):
        d = decay[n]
        m = gmap[...]
        r = dn(readers[n, C:], m, 1, 0)
        gmap[...] = jnp.concatenate(
            [d * m[:, :C] - r[:, :C] + added[n], d * m[:, C:] - r[:, C:]], 1
        )
        return carry

    lax.fori_loop(0, CHUNKS, grow, 0)
    rowmaps[py] = gmap[...]
    row_copies = go([
        remote(f"r{t}", gmap, rowmaps.at[py], along_row(t)) for t in (1, 3, 2)
    ])
    each(far_on, 0)
    each(crossed_one, 1)
    first_hop()
    arrive(row_copies)
    whole = rowmaps[0]
    for t in range(1, SIDE):
        m = rowmaps[t]
        whole = dot3(m[:, C:], whole)
        whole = jnp.concatenate([whole[:, :C] + m[:, :C], whole[:, C:]], 1)
    colmaps[px] = whole
    col_copies = go([
        remote(f"c{t}", colmaps.at[px], colmaps.at[px], along_column(t)) for t in (1, 3, 2)
    ])
    each(near_on, 1)
    each(far, 1)
    pass_on(1)
    each(complete, 0)
    merge(gs, 0, wg, GATE_KINDS)
    merge(us, 0, wu, UP_KINDS)
    share_own = share("g", wg, 0) + share("u", wu, 0) + share("d", wd, 0)
    arrive(col_copies)
    entering = s0_ref[0]
    for t in range(SIDE - 1):
        m = colmaps[t]
        entering = jnp.where(px > t, dot3(m[:, C:], entering) + m[:, :C], entering)
    for t in range(SIDE - 1):
        m = rowmaps[t]
        entering = jnp.where(py > t, dot3(m[:, C:], entering) + m[:, :C], entering)
    state[...] = entering
    pass_on(2)
    each(far_on, 1)
    gather(1)
    arrive(share_own)
    ROWS = WINDOW * CAP
    experts(0, 2, ROWS // 2, ROWS)
    pass_on(3)
    lax.fori_loop(0, CHUNKS, outputs, 0)
    state_ref[0, 0] = state[...]
    complete(("g", 1))
    merge(gs, 1, wg, GATE_KINDS)
    share_gate = share("g", wg, 1)
    complete(("u0", 1))
    complete(("u1", 1))
    merge(us, 1, wu, UP_KINDS)
    share_up = share("u", wu, 1)
    complete(("d", 1))
    share_down = share("d", wd, 1)
    pass_on(4)
    gather(0)
    experts(0, 2, 0, ROWS // 2)
    experts(2, 3, 0, ROWS)
    arrive(share_gate + share_up + share_down)
    experts(3, 4, 0, ROWS)
    combine(0)

    sums = {}

    def send_sum(distance):
        way = -1 if distance > 0 else 1
        at = SLOT[distance]
        for half in range(2):
            part = pl.ds(half * (TOK // 2), TOK // 2)
            if distance in (4, -3):
                src = contrib.at[at, part]
            else:
                arrive(sums[distance - way, half])
                inbox = SLOT[distance - way]
                rs_out[at, part, :] = (
                    contrib[at, part, :].astype(F32) + rs_in[inbox, part, :].astype(F32)
                ).astype(BF)
                src = rs_out.at[at, part]
            sums[distance, half] = go([
                remote(f"s{distance}{half}", src, rs_in.at[at, part], along_z(way))
            ])

    send_sum(4)
    send_sum(-3)
    combine(1)

    send_sum(3)
    send_sum(-2)
    send_sum(2)
    send_sum(-1)
    send_sum(1)
    for half in range(2):
        part = pl.ds(half * (TOK // 2), TOK // 2)
        arrive(sums[-1, half] + sums[1, half])
        mix_ref[part, :] = (
            contrib[SLOT[0], part, :].astype(F32)
            + rs_in[SLOT[1], part, :].astype(F32)
            + rs_in[SLOT[-1], part, :].astype(F32)
        ).astype(BF)
    for one in started:
        one.wait_send()


COPIES = 4 + 48 + 21 + 6 + 6 + 14


def on_device(
    q, k, v, strength, rate, factor, extra, s0, residual, seg, routes, gain, router, gate, up, down
):
    vmem = pl.BlockSpec(memory_space=pltpu.VMEM)
    hbm = pl.BlockSpec(memory_space=pl.ANY)
    V = pltpu.VMEM
    return pl.pallas_call(
        kernel,
        out_shape=(
            jax.ShapeDtypeStruct((CHUNKS * C, C), BF),
            jax.ShapeDtypeStruct((1, 1, C, C), F32),
            jax.ShapeDtypeStruct((TOK, D), BF),
        ),
        in_specs=[vmem] * 13 + [hbm] * 3,
        out_specs=(vmem, vmem, vmem),
        scratch_shapes=[
            V((2, SHARDS, DEPTH, FE), BF),
            V((2, SHARDS, DEPTH, FE), BF),
            V((LOCAL, D, FE), BF),
            V((LOCAL, D, FE), BF),
            V((LOCAL, FE, D), BF),
            V((WINDOW, TOK, D), BF),
            V((WINDOW, EXPERTS, TOK), BF),
            V((WINDOW, 8, TOK), F32),
            V((WINDOW, 8, TOK), F32),
            V((LOCAL, WINDOW * CAP, D), BF),
            V((LOCAL, WINDOW * CAP, D), BF),
            V((WINDOW, TOK, D), BF),
            V((WINDOW, TOK, D), BF),
            V((WINDOW, TOK, D), BF),
            V((CHUNKS, 2 * C, C), BF),
            V((CHUNKS, C, C), F32),
            V((CHUNKS, C, C), F32),
            V((CHUNKS, C, C), F32),
            V((C, 2 * C), F32),
            V((SIDE, C, 2 * C), F32),
            V((SIDE, C, 2 * C), F32),
            V((C, C), F32),
            pltpu.SemaphoreType.DMA((COPIES,)),
            pltpu.SemaphoreType.DMA((COPIES,)),
            pltpu.SemaphoreType.DMA((4,)),
        ],
        compiler_params=pltpu.CompilerParams(
            collective_id=0, has_side_effects=True, vmem_limit_bytes=58 << 20
        ),
        cost_estimate=pl.CostEstimate(
            flops=7_000_000_000, bytes_accessed=6_000_000, transcendentals=2_000_000
        ),
    )(
        q, k, v,
        strength.reshape(CHUNKS, C), rate, factor.reshape(CHUNKS, C), extra.reshape(CHUNKS, C),
        s0, residual, seg.reshape(1, TOK), routes, gain, router, gate, up, down,
    )


def solution(mesh):
    placed = (
        P("ctx", "exp"), P("ctx", "exp"), P("ctx", "exp"), P("exp", "ctx"), P("exp", None),
        P("exp", "ctx"), P("exp", "ctx"), P("exp", None, None), P(("ctx", "exp"), None),
        P(("ctx", "exp")), P(("ctx", "exp"), None), P(), P(),
        P("exp", "ctx", None), P("exp", "ctx", None), P("exp", "ctx", None),
    )
    return jax.shard_map(
        on_device,
        mesh=mesh,
        in_specs=placed,
        out_specs=(P("ctx", "exp"), P("ctx", "exp", None, None), P(("ctx", "exp"), None)),
        check_vma=False,
    )
```

time: 144 us -> 115 us (0.80); the launches traced: 142 us -> 115 us
  Pallas kernels: 136 us -> 108 us
    pallas_call x1, Pallas kernels: 136 us -> 108 us  [on_device(): pl.pallas_call(kernel, out_shape=(jax.ShapeDtypeStruct((CHUNKS * C, C), B...]
where the time goes in v2:
time: 115 us
  Pallas kernels  108 us (94%)
  local copies, waits for them, and re-layouts  5.41 us (5%)
    pallas_call x1, Pallas kernels, on_device(): pl.pallas_call(kernel, out_shape=(jax.ShapeDtypeStruct((CHUNKS * C, C), B...  108 us
    unnamed x11, local copies, waits for them, and re-layouts  5.41 us

profile of v2, /device:TPU:1, one launch (start us, length us, event | category | flops | bytes accessed | tf_op | source)
XLA Modules:
  0.0 114.5 jit_solution(6648847256612352034)
XLA Ops:
  0.6 0.0 copy-start.1
  0.6 1.4 %copy.19.routes_ref = s32[128,8]{1,0:T(8,128)} copy(s32[128,8]{0,1:T(8,128)} %param.26) | data formatting | bytes 8192 | tf_op args[10]
  2.1 0.0 copy-done.1
  2.1 0.9 copy.20.router_ref
  3.0 108.5 %shard_map.175 = (bf16[1024,128]{1,0:T(8,128)(2,1)}, f32[1,1,128,128]{3,2,1,0:T(8,128)}, bf16[128,1152]{1,0:T(8,128)(2,1)}) custom-call(bf16[1024,128]{1,0:T(8,128)(2,1)} %q_ref.1, bf16[1024,128]{1,0:T(8,128)(2,1)} %k_ref.1, bf16[1024,128]{1,0:T(8,128)(2,1)} %v_ref.1, f32[8,128]{1,0:T(8,128)} %bitcast.4, f32[1,128]{1,0:T(1,128)} %rate_ref.1, ...), custom_call_target="tpu_custom_call" | custom-call | flops 7000000000 | bytes 6000000 | tf_op jit(solution)/shard_map/pallas_call | solution.py:531
  111.5 0.0 copy-start.2
  111.5 0.0 copy-start
  111.5 1.7 %copy.24 = bf16[1024,128]{1,0:T(8,128)(2,1)} copy(bf16[1024,128]{1,0:T(8,128)(2,1)} %get-tuple-element.6) | data formatting | bytes 524288
  113.2 0.0 copy-done.2
  113.2 0.6 copy.25
  113.8 0.0 copy-done
  113.8 0.7 copy.26
Async XLA Ops:
  0.6 1.5 %copy-start.1 = (bf16[1152,32]{0,1:T(8,128)(2,1)S(1)}, bf16[1152,32]{0,1:T(8,128)(2,1)}, u32[]{:S(2)}) copy-start(bf16[1152,32]{0,1:T(8,128)(2,1)} %param.28) | copy-start | bytes 221188
  111.5 1.7 %copy-start.2 = (f32[1,1,128,128]{3,2,1,0:T(8,128)S(1)}, f32[1,1,128,128]{3,2,1,0:T(8,128)}, u32[]{:S(2)}) copy-start(f32[1,1,128,128]{3,2,1,0:T(8,128)} %get-tuple-element.7) | copy-start | bytes 196612
  111.5 2.4 %copy-start = (bf16[128,1152]{1,0:T(8,128)(2,1)S(1)}, bf16[128,1152]{1,0:T(8,128)(2,1)}, u32[]{:S(2)}) copy-start(bf16[128,1152]{1,0:T(8,128)(2,1)} %get-tuple-element.8) | copy-start | bytes 884740

commit v3 on v2

--- a/solution.py
+++ b/solution.py
@@ -265,16 +265,14 @@
     )
     normed = (stream * scale * gains).astype(BF)
     tok[SLOT[0]] = normed
-    logits = dn(normed, router_ref[...], 1, 0)
-    lane = lax.broadcasted_iota(jnp.int32, (TOK, EXPERTS), 1)
-    hits = jnp.zeros((TOK, EXPERTS), F32)
-    routes = routes_ref[...]
+    logits = dn(router_ref[...], normed, 1, 1)
+    expert = lax.broadcasted_iota(jnp.int32, (EXPERTS, TOK), 0)
+    hits = jnp.zeros((EXPERTS, TOK), F32)
     for turn in range(8):
-        hits = hits + jnp.where(routes[:, turn : turn + 1] == lane, 1.0, 0.0)
+        hits = hits + jnp.where(routes_ref[turn : turn + 1, :] == expert, 1.0, 0.0)
     scores = jnp.where(hits > 0.0, 1.0 / (1.0 + jnp.exp(-logits)), 0.0)
-    weights = route_scale * scores / jnp.sum(scores, axis=1, keepdims=True)
-    wide = jnp.concatenate([weights, jnp.zeros((TOK, C - EXPERTS), F32)], 1)
-    table[SLOT[0]] = jnp.transpose(wide)[:EXPERTS].astype(BF)
+    weights = route_scale * scores / jnp.sum(scores, axis=0, keepdims=True)
+    table[SLOT[0]] = weights.astype(BF)
 
     def token_step(way, k, half):
         src, dst = SLOT[way * (k - 1)], SLOT[way * k]
@@ -334,7 +332,7 @@
     def outputs(n, carry):
         s = state[...]
         r = dn(readers[n], s, 1, 0)
-        att_ref[pl.ds(pl.multiple_of(n * C, C), C), :] = (inner[n] + r[:C]).astype(BF)
+        att_ref[pl.ds(pl.multiple_of(n * C, C), C), :] = inner[n] + r[:C]
         state[...] = decay[n] * s - r[C:] + added[n]
         return carry
 
@@ -472,10 +470,9 @@
     share_down = share("d", wd, 1)
     pass_on(4)
     gather(0)
-    experts(0, 2, 0, ROWS // 2)
-    experts(2, 3, 0, ROWS)
+    experts(0, 3, 0, ROWS // 2)
     arrive(share_gate + share_up + share_down)
-    experts(3, 4, 0, ROWS)
+    experts(3, 4, 0, ROWS // 2)
     combine(0)
 
     sums = {}
@@ -500,6 +497,7 @@
 
     send_sum(4)
     send_sum(-3)
+    experts(2, 4, ROWS // 2, ROWS)
     combine(1)
 
     send_sum(3)
@@ -528,10 +526,10 @@
     vmem = pl.BlockSpec(memory_space=pltpu.VMEM)
     hbm = pl.BlockSpec(memory_space=pl.ANY)
     V = pltpu.VMEM
-    return pl.pallas_call(
+    attended, ends, mixed = pl.pallas_call(
         kernel,
         out_shape=(
-            jax.ShapeDtypeStruct((CHUNKS * C, C), BF),
+            jax.ShapeDtypeStruct((CHUNKS * C, C), F32),
             jax.ShapeDtypeStruct((1, 1, C, C), F32),
             jax.ShapeDtypeStruct((TOK, D), BF),
         ),
@@ -573,8 +571,9 @@
     )(
         q, k, v,
         strength.reshape(CHUNKS, C), rate, factor.reshape(CHUNKS, C), extra.reshape(CHUNKS, C),
-        s0, residual, seg.reshape(1, TOK), routes, gain, router, gate, up, down,
+        s0, residual, seg.reshape(1, TOK), routes.T, gain, router.T, gate, up, down,
     )
+    return attended.astype(BF), ends, mixed
 
 
 def solution(mesh):

time: 115 us -> 111 us (0.965)
  local copies, waits for them, and re-layouts: 5.41 us -> 1.35 us
  other arithmetic: 0 us -> 1.82 us
    unnamed x11 -> x6, local copies, waits for them, and re-layouts: 5.41 us -> 1.35 us
    convert_element_type x0 -> x1, other arithmetic: none -> 1.82 us  [on_device(): return (attended.astype(BF), ends, mixed)]
where the time goes in v3:
time: 111 us
  Pallas kernels  107 us (96%)
  other arithmetic  1.82 us (2%)
  local copies, waits for them, and re-layouts  1.35 us (1%)
    pallas_call x1, Pallas kernels, on_device(): pl.pallas_call(kernel, out_shape=(jax.ShapeDtypeStruct((CHUNKS * C, C), F...  107 us

profile of v3, /device:TPU:1, one launch (start us, length us, event | category | flops | bytes accessed | tf_op | source)
XLA Modules:
  0.0 111.3 jit_solution(6947055530730974548)
XLA Ops:
  0.6 107.5 %shard_map.175 = (f32[1024,128]{1,0:T(8,128)}, f32[1,1,128,128]{3,2,1,0:T(8,128)}, bf16[128,1152]{1,0:T(8,128)(2,1)}) custom-call(bf16[1024,128]{1,0:T(8,128)(2,1)} %q_ref.1, bf16[1024,128]{1,0:T(8,128)(2,1)} %k_ref.1, bf16[1024,128]{1,0:T(8,128)(2,1)} %v_ref.1, f32[8,128]{1,0:T(8,128)} %bitcast.7, f32[1,128]{1,0:T(1,128)} %rate_ref.1, f32[8,128]{1,0:T(8,128)} %bitcast.8, ...), custom_call_target="tpu_custom_call" | custom-call | flops 7000000000 | bytes 6000000 | tf_op jit(solution)/shard_map/pallas_call | solution.py:529
  108.1 0.0 copy-start.1
  108.1 0.0 copy-start
  108.1 1.8 %convert_element_type.3 = bf16[1024,128]{1,0:T(8,128)(2,1)} convert(f32[1024,128]{1,0:T(8,128)} %get-tuple-element.6) | non-fusion elementwise | flops 131072 | bytes 786432 | tf_op jit(solution)/shard_map/convert_element_type | solution.py:576
  109.9 0.0 copy-done.1
  109.9 0.6 copy.21
  110.6 0.0 copy-done
  110.6 0.7 copy.22
Async XLA Ops:
  108.1 1.8 %copy-start.1 = (f32[1,1,128,128]{3,2,1,0:T(8,128)S(1)}, f32[1,1,128,128]{3,2,1,0:T(8,128)}, u32[]{:S(2)}) copy-start(f32[1,1,128,128]{3,2,1,0:T(8,128)} %get-tuple-element.13) | copy-start | bytes 196612
  108.1 2.5 %copy-start = (bf16[128,1152]{1,0:T(8,128)(2,1)S(1)}, bf16[128,1152]{1,0:T(8,128)(2,1)}, u32[]{:S(2)}) copy-start(bf16[128,1152]{1,0:T(8,128)(2,1)} %get-tuple-element.14) | copy-start | bytes 884740

commit v4 on v3

--- a/solution.py
+++ b/solution.py
@@ -102,11 +102,12 @@
 
 
 def kernel(
-    q_ref, k_ref, v_ref, b_ref, rate_ref, f_ref, x_ref, s0_ref, res_ref, seg_ref, routes_ref,
+    q_hbm, k_hbm, v_hbm, b_ref, rate_ref, f_ref, x_ref, s0_hbm, res_hbm, seg_ref, routes_ref,
     gain_ref, router_ref, gate_ref, up_ref, down_ref,
     att_ref, state_ref, mix_ref,
     gs, us, wg, wu, wd, tok, table, slot_ids, slot_w, xin, eo, contrib, rs_out,
-    rs_in, readers, inner, added, decay, gmap, rowmaps, colmaps, state, send_sem, recv_sem, loc_sem,
+    rs_in, readers, inner, added, decay, gmap, rowmaps, colmaps, state,
+    q_ref, k_ref, v_ref, s0_ref, res_ref, send_sem, recv_sem, loc_sem,
 ):
     ctx = lax.axis_index("ctx")
     own = lax.axis_index("exp")
@@ -151,6 +152,15 @@
     def arrive(copies):
         for one in copies:
             one.wait_recv()
+
+    reads = [
+        pltpu.make_async_copy(src, dst, loc_sem.at[4 + n])
+        for n, (src, dst) in enumerate((
+            (res_hbm, res_ref), (q_hbm, q_ref), (k_hbm, k_ref), (v_hbm, v_ref), (s0_hbm, s0_ref),
+        ))
+    ]
+    for one in reads:
+        one.start()
 
     barrier = pltpu.get_barrier_semaphore()
     partners = [along_z(t) for t in (1, -1, 8)] + [sibling]
@@ -252,6 +262,8 @@
         arrive(across[key[0]])
         near(key)
 
+    for one in reads:
+        one.wait()
     row, col = iotas((C, C))
     stream = res_ref[...].astype(F32)
     scale = lax.rsqrt(jnp.mean(stream * stream, axis=1, keepdims=True) + norm_eps)
@@ -533,7 +545,7 @@
             jax.ShapeDtypeStruct((1, 1, C, C), F32),
             jax.ShapeDtypeStruct((TOK, D), BF),
         ),
-        in_specs=[vmem] * 13 + [hbm] * 3,
+        in_specs=[hbm] * 3 + [vmem] * 4 + [hbm] * 2 + [vmem] * 4 + [hbm] * 3,
         out_specs=(vmem, vmem, vmem),
         scratch_shapes=[
             V((2, SHARDS, DEPTH, FE), BF),
@@ -558,9 +570,14 @@
             V((SIDE, C, 2 * C), F32),
             V((SIDE, C, 2 * C), F32),
             V((C, C), F32),
+            V((CHUNKS * C, C), BF),
+            V((CHUNKS * C, C), BF),
+            V((CHUNKS * C, C), BF),
+            V((1, C, C), F32),
+            V((TOK, D), BF),
             pltpu.SemaphoreType.DMA((COPIES,)),
             pltpu.SemaphoreType.DMA((COPIES,)),
-            pltpu.SemaphoreType.DMA((4,)),
+            pltpu.SemaphoreType.DMA((9,)),
         ],
         compiler_params=pltpu.CompilerParams(
             collective_id=0, has_side_effects=True, vmem_limit_bytes=58 << 20

time: 111 us -> 111 us (level)
  no operation moved by 1% of the time
where the time goes in v4:
time: 111 us
  Pallas kernels  107 us (96%)
  other arithmetic  1.82 us (2%)
  local copies, waits for them, and re-layouts  1.35 us (1%)
    pallas_call x1, Pallas kernels, on_device(): pl.pallas_call(kernel, out_shape=(jax.ShapeDtypeStruct((CHUNKS * C, C), F...  107 us

profile of v4, /device:TPU:1, one launch (start us, length us, event | category | flops | bytes accessed | tf_op | source)
XLA Modules:
  0.0 111.0 jit_solution(17400229470434671606)
XLA Ops:
  0.6 107.2 %shard_map.175 = (f32[1024,128]{1,0:T(8,128)}, f32[1,1,128,128]{3,2,1,0:T(8,128)}, bf16[128,1152]{1,0:T(8,128)(2,1)}) custom-call(bf16[1024,128]{1,0:T(8,128)(2,1)} %q_hbm.1, bf16[1024,128]{1,0:T(8,128)(2,1)} %k_hbm.1, bf16[1024,128]{1,0:T(8,128)(2,1)} %v_hbm.1, f32[8,128]{1,0:T(8,128)} %bitcast.7, f32[1,128]{1,0:T(1,128)} %rate_ref.1, f32[8,128]{1,0:T(8,128)} %bitcast.8, ...), custom_call_target="tpu_custom_call" | custom-call | flops 7000000000 | bytes 6000000 | tf_op jit(solution)/shard_map/pallas_call | solution.py:541
  107.9 0.0 copy-start.1
  107.9 0.0 copy-start
  107.9 1.8 %convert_element_type.3 = bf16[1024,128]{1,0:T(8,128)(2,1)} convert(f32[1024,128]{1,0:T(8,128)} %get-tuple-element.6) | non-fusion elementwise | flops 131072 | bytes 786432 | tf_op jit(solution)/shard_map/convert_element_type | solution.py:593
  109.7 0.0 copy-done.1
  109.7 0.6 copy.21
  110.3 0.0 copy-done
  110.3 0.7 copy.22
Async XLA Ops:
  107.9 1.8 %copy-start.1 = (f32[1,1,128,128]{3,2,1,0:T(8,128)S(1)}, f32[1,1,128,128]{3,2,1,0:T(8,128)}, u32[]{:S(2)}) copy-start(f32[1,1,128,128]{3,2,1,0:T(8,128)} %get-tuple-element.13) | copy-start | bytes 196612
  107.9 2.5 %copy-start = (bf16[128,1152]{1,0:T(8,128)(2,1)S(1)}, bf16[128,1152]{1,0:T(8,128)(2,1)}, u32[]{:S(2)}) copy-start(bf16[128,1152]{1,0:T(8,128)(2,1)} %get-tuple-element.14) | copy-start | bytes 884740
